TPU v7x, 32 devices: a whole 2x2x4 slice. The times are simulated.
32 devices in a mesh: head: 4 (over x, core), blk: 8 (over z, y).
Axes of the slice: x: 2, y: 2, z: 4, core: 2. Of those that a mesh axis runs over, the one named last changes fastest.
Arguments:
- tokens: bfloat16 [2048, 4, 768], P('blk', 'head'), may hold values from -6 to 6
- attn_gain: bfloat16 [768], P(('head', 'blk')), may hold values from 0.5 to 1.5
- w_query: bfloat16 [768, 768], P(('head', 'blk')), may hold values from -0.109375 to 0.109375
- w_key: bfloat16 [768, 768], P(('head', 'blk')), may hold values from -0.109375 to 0.109375
- w_value: bfloat16 [768, 768], P(('head', 'blk')), may hold values from -0.21875 to 0.21875
- w_out: bfloat16 [768, 768], P(None, ('head', 'blk')), may hold values from -0.875 to 0.875
- bias_table: bfloat16 [384], P(('head', 'blk')), may hold values from -3 to 3
- moe_gain: bfloat16 [768], P(('head', 'blk')), may hold values from 0.5 to 1.5
- w_router: bfloat16 [768, 8], P(('head', 'blk')), may hold values from -0.15625 to 0.15625
- expert_in: bfloat16 [8, 768, 3072], P('blk', None, 'head'), may hold values from -0.21875 to 0.21875
- expert_out: bfloat16 [8, 3072, 768], P('blk', 'head'), may hold values from -0.875 to 0.875
- seq_lengths: int32 [4], replicated, may hold values from 1024 to 2048, as said below
- rel_buckets: int32 [2048], replicated, may hold values from 0 to 31, as said below
- routes: int32 [4, 2048, 1, 1], P('head', 'blk'), may hold values from 0 to 7; in each aligned block of 256 rows (0 to 255, 256 to 511, ..., all dimensions but the last counted through in order) at most 48 rows name the same one
- cotangent: bfloat16 [2048, 4, 768], P('blk', 'head'), may hold values from -6 to 6
Outputs:
- result: bfloat16 [2048, 4, 768], P('blk', 'head')
- grad_tokens: float32 [2048, 4, 768], P('blk', 'head')
- grad_attn_gain: float32 [768], P(('head', 'blk'))
- grad_query: float32 [768, 768], P(('head', 'blk'))
- grad_key: float32 [768, 768], P(('head', 'blk'))
- grad_value: float32 [768, 768], P(('head', 'blk'))
- grad_out: float32 [768, 768], P(None, ('head', 'blk'))
- grad_table: float32 [384], P(('head', 'blk'))
- grad_moe_gain: float32 [768], P(('head', 'blk'))
- grad_router: float32 [768, 8], P(('head', 'blk'))
- grad_expert_in: float32 [8, 768, 3072], P('blk', None, 'head')
- grad_expert_out: float32 [8, 3072, 768], P('blk', 'head')
Inputs may be any that keep to these rules, and one draw needn't show every extreme that they name: `seq_lengths`: one sequence, which one drawn from the seed, has exactly 2048 tokens. `rel_buckets`: entry j is the bucket of distance j: j itself for j below half of 32, never falling, and 31 at the last entry. `routes`: in each aligned block of 256 rows (the rows of one device, in the array's order) no expert is named more than 48 times; in some blocks one expert is named exactly 48 times.
All inputs are finite; a program needn't handle non-finite values.
Results may differ from a plain program's by a relative error of at most 0.02.
Values may be sent and summed in bfloat16 or wider, within the bound.
No kernel may reach another device: no remote copies, remote signals or barrier semaphores. Data moves between devices by JAX's collectives and lax.ppermute only.
A program may use at most 256 MiB of HBM per device.

v0:
```python
import math

import jax
import jax.numpy as jnp
from jax import lax
from jax.sharding import PartitionSpec as P

HEADS = 12
HEAD_DIM = 64
NUM_BUCKETS = 32


norm_eps = 1e-06
masked_score = -1e30


def inverse_rms(values):
    return lax.rsqrt(jnp.mean(values * values, axis=-1, keepdims=True) + norm_eps)


def norm_backward(grad_normed, source, inv_scale, gain):
    weighted = grad_normed * gain
    inner_mean = jnp.mean(weighted * source, axis=-1, keepdims=True)
    grad_source = inv_scale * weighted - source * (inv_scale * inv_scale * inv_scale) * inner_mean
    grad_gain = jnp.sum(grad_normed * source * inv_scale, axis=0)
    return (grad_source, grad_gain)


def same_state(running):
    return running


def bucket_bounds(rel_buckets):
    bucket_count = NUM_BUCKETS
    labels = jnp.arange(bucket_count, dtype=jnp.int32)
    starts = jnp.sum((rel_buckets[:, None] < labels[None, :]).astype(jnp.int32), axis=0)
    ends = jnp.concatenate([starts[1:], jnp.full((1,), rel_buckets.shape[0] + 1, jnp.int32)])
    return (starts, ends)


def bias_terms(query_positions, key_positions, bounds, table32):
    starts, ends = bounds
    distance = jnp.maximum(query_positions[:, None] - key_positions[None, :], 0)[:, :, None]
    inside = (distance >= starts[None, None, :]) & (distance < ends[None, None, :])
    onehot = inside.astype(jnp.bfloat16)
    bias = jnp.einsum(
        "qkb,bh->hqk", onehot, table32.astype(jnp.bfloat16), preferred_element_type=jnp.float32
    )
    return (onehot, bias)


def block_scores(queries, keys, query_positions, key_positions, seq_lengths, bounds, table32):
    onehot, bias = bias_terms(query_positions, key_positions, bounds, table32)
    raw = jnp.einsum("qshd,kshd->hsqk", queries, keys, preferred_element_type=jnp.float32)
    causal = key_positions[None, :] <= query_positions[:, None]
    present = key_positions[None, :] < seq_lengths[:, None]
    valid = causal[None, :, :] & present[:, None, :]
    return (raw + bias[:, None, :, :], valid[None], onehot)


def attend_step(
    running, queries, keys, values, query_positions, key_positions, seq_lengths, bounds, table32
):
    row_top, row_total, weighted = running
    scores, valid, unused = block_scores(
        queries, keys, query_positions, key_positions, seq_lengths, bounds, table32
    )
    scores = jnp.where(valid, scores, masked_score)
    new_top = jnp.maximum(row_top, jnp.max(scores, axis=-1))
    weights = jnp.where(valid, jnp.exp(scores - new_top[..., None]), 0.0)
    decay = jnp.exp(row_top - new_top)
    row_total = row_total * decay + jnp.sum(weights, axis=-1)
    mixed = jnp.einsum(
        "hsqk,kshd->qshd", weights.astype(jnp.bfloat16), values, preferred_element_type=jnp.float32
    )
    weighted = weighted * jnp.transpose(decay, (2, 1, 0))[..., None] + mixed
    return (new_top, row_total, weighted)


def grad_step(
    queries,
    grad_heads,
    log_total,
    delta,
    query_positions,
    keys,
    values,
    key_positions,
    seq_lengths,
    bounds,
    table32,
):
    scores, valid, onehot = block_scores(
        queries, keys, query_positions, key_positions, seq_lengths, bounds, table32
    )
    probs = jnp.where(valid, jnp.exp(scores - jnp.transpose(log_total, (2, 1, 0))[..., None]), 0.0)
    grad_probs = jnp.einsum(
        "qshd,kshd->hsqk", grad_heads, values, preferred_element_type=jnp.float32
    )
    grad_scores = probs * (grad_probs - jnp.transpose(delta, (2, 1, 0))[..., None])
    grad_table = jnp.einsum(
        "hqk,qkb->bh",
        jnp.sum(grad_scores, axis=1),
        onehot.astype(jnp.float32),
        precision=lax.Precision.HIGHEST,
    )
    low_scores = grad_scores.astype(jnp.bfloat16)
    grad_queries = jnp.einsum(
        "hsqk,kshd->qshd", low_scores, keys, preferred_element_type=jnp.float32
    )
    grad_keys = jnp.einsum(
        "hsqk,qshd->kshd", low_scores, queries, preferred_element_type=jnp.float32
    )
    grad_values = jnp.einsum(
        "hsqk,qshd->kshd",
        probs.astype(jnp.bfloat16),
        grad_heads,
        preferred_element_type=jnp.float32,
    )
    return (grad_queries, grad_keys, grad_values, grad_table)


def on_device(
    tokens,
    attn_gain,
    w_query,
    w_key,
    w_value,
    w_out,
    bias_table,
    moe_gain,
    w_router,
    expert_in,
    expert_out,
    seq_lengths,
    rel_buckets,
    routes,
    cotangent,
):
    head_count = lax.axis_size("head")
    blk_count = lax.axis_size("blk")
    head_index = lax.axis_index("head")
    blk_index = lax.axis_index("blk")
    block_rows, group_seqs, width = tokens.shape
    seq_count = group_seqs * head_count
    tok_rows = block_rows * group_seqs
    local_heads = HEADS // head_count
    head_width = local_heads * HEAD_DIM
    group_rows = block_rows * max(1, blk_count // 8)
    longest = jnp.max(seq_lengths)
    query_first = blk_index * block_rows
    query_last = query_first + block_rows - 1
    query_positions = query_first + jnp.arange(block_rows, dtype=jnp.int32)
    bounds = bucket_bounds(rel_buckets)
    fetched = (
        lax.all_gather(w_query, ("head", "blk"), axis=0, tiled=True),
        lax.all_gather(w_key, ("head", "blk"), axis=0, tiled=True),
        lax.all_gather(w_value, ("head", "blk"), axis=0, tiled=True),
        lax.all_gather(w_out, ("head", "blk"), axis=1, tiled=True),
        lax.all_gather(attn_gain, ("head", "blk"), axis=0, tiled=True),
        lax.all_gather(bias_table, ("head", "blk"), axis=0, tiled=True),
        lax.all_gather(moe_gain, ("head", "blk"), axis=0, tiled=True),
        lax.all_gather(w_router, ("head", "blk"), axis=0, tiled=True),
    )
    full_query, full_key, full_value, full_out, gain_attn, table_flat, gain_moe, full_router = (
        fetched
    )
    inner_width = full_query.shape[1]
    table_all = table_flat.astype(jnp.float32).reshape(NUM_BUCKETS, HEADS)
    table32 = lax.dynamic_slice_in_dim(table_all, head_index * local_heads, local_heads, 1)
    gain_attn32 = gain_attn.astype(jnp.float32)
    gain_moe32 = gain_moe.astype(jnp.float32)

    def to_heads(values):
        parts = values.shape[1]
        shaped = values.reshape(block_rows, group_seqs, parts, head_count, head_width)
        moved = lax.all_to_all(shaped, "head", split_axis=3, concat_axis=1, tiled=True)
        return moved.reshape(block_rows, seq_count, parts, local_heads, HEAD_DIM)

    def to_tokens(values):
        parts = values.shape[2]
        shaped = values.reshape(block_rows, seq_count, parts, 1, head_width)
        moved = lax.all_to_all(shaped, "head", split_axis=1, concat_axis=3, tiled=True)
        return moved.reshape(tok_rows, parts, inner_width)

    source = tokens.astype(jnp.float32).reshape(tok_rows, width)
    inv_attn = inverse_rms(source)
    attn_in = (source * inv_attn * gain_attn32).astype(jnp.bfloat16)
    stacked_weights = jnp.stack((full_query, full_key, full_value))
    projected = jnp.einsum(
        "td,cde->tce", attn_in, stacked_weights, preferred_element_type=jnp.float32
    ).astype(jnp.bfloat16)
    heads_in = to_heads(projected)
    queries = heads_in[:, :, 0]
    keys = heads_in[:, :, 1]
    values = heads_in[:, :, 2]
    start_state = (
        jnp.full((local_heads, seq_count, block_rows), masked_score, jnp.float32),
        jnp.zeros((local_heads, seq_count, block_rows), jnp.float32),
        jnp.zeros((block_rows, seq_count, local_heads, HEAD_DIM), jnp.float32),
    )
    key_piece = lax.all_gather(keys, "blk", axis=0, tiled=True)
    value_piece = lax.all_gather(values, "blk", axis=0, tiled=True)
    piece_rows = key_piece.shape[0]
    part_rows = math.gcd(piece_rows, group_rows)

    def forward_one_part(step_index, inner_state):
        offset = step_index * part_rows
        key_part = lax.dynamic_slice_in_dim(key_piece, offset, part_rows, 0)
        value_part = lax.dynamic_slice_in_dim(value_piece, offset, part_rows, 0)
        key_positions = offset + jnp.arange(part_rows, dtype=jnp.int32)

        def attend_now(current):
            return attend_step(
                current,
                queries,
                key_part,
                value_part,
                query_positions,
                key_positions,
                seq_lengths,
                bounds,
                table32,
            )

        skipped = (offset > query_last) | (offset >= longest)
        return lax.cond(skipped, same_state, attend_now, inner_state)

    row_top, row_total, weighted = lax.fori_loop(
        0, piece_rows // part_rows, forward_one_part, start_state
    )
    attn_heads = (weighted / jnp.transpose(row_total, (2, 1, 0))[..., None]).astype(jnp.bfloat16)
    log_total = jnp.transpose(row_top + jnp.log(row_total), (2, 1, 0))
    attn_tok = to_tokens(attn_heads[:, :, None])[:, 0]
    branch = jnp.dot(attn_tok, full_out, preferred_element_type=jnp.float32)
    hidden = source + branch
    expert_count = full_router.shape[1]
    local_experts = expert_in.shape[0]
    capacity = max(2, 3 * tok_rows // (2 * expert_count))
    inv_moe = inverse_rms(hidden)
    moe_in = (hidden * inv_moe * gain_moe32).astype(jnp.bfloat16)
    logits = jnp.dot(moe_in, full_router, preferred_element_type=jnp.float32)
    router_probs = jax.nn.softmax(logits, axis=-1)
    route_flat = routes.reshape(tok_rows)
    chosen = route_flat[:, None] == jnp.arange(expert_count, dtype=jnp.int32)[None, :]
    gate = jnp.sum(jnp.where(chosen, router_probs, 0.0), axis=-1)
    filled = jnp.cumsum(chosen.astype(jnp.int32), axis=0)
    slot = jnp.sum(jnp.where(chosen, filled - 1, 0), axis=-1)
    target = route_flat * capacity + slot
    dispatch = (
        target[:, None] == jnp.arange(expert_count * capacity, dtype=jnp.int32)[None, :]
    ).astype(jnp.bfloat16)

    def to_buffer(token_rows):
        packed = jnp.einsum(
            "tj,td->jd", dispatch, token_rows, preferred_element_type=jnp.float32
        ).astype(jnp.bfloat16)
        return packed.reshape(blk_count, local_experts, capacity, width)

    def from_buffer(buffer):
        return jnp.dot(
            dispatch,
            buffer.reshape(expert_count * capacity, width),
            preferred_element_type=jnp.float32,
        )

    def to_experts(buffer):
        return lax.all_to_all(buffer, "blk", split_axis=0, concat_axis=0, tiled=True)

    def all_rows(buffer):
        return lax.all_gather(buffer, "head", axis=0, tiled=True)

    def summed_rows(partial_terms):
        return lax.psum_scatter(
            partial_terms.astype(jnp.bfloat16), "head", scatter_dimension=0, tiled=True
        ).astype(jnp.float32)

    def to_owners(buffer):
        return lax.all_to_all(buffer, "blk", split_axis=0, concat_axis=0, tiled=True)

    expert_rows_in = all_rows(to_experts(to_buffer(moe_in)))
    expert_pre = jnp.einsum(
        "necd,edf->necf", expert_rows_in, expert_in, preferred_element_type=jnp.float32
    )
    expert_act, gelu_pull = jax.vjp(jax.nn.gelu, expert_pre)
    expert_low = expert_act.astype(jnp.bfloat16)
    expert_terms = jnp.einsum(
        "necf,efd->necd", expert_low, expert_out, preferred_element_type=jnp.float32
    )
    expert_tok = from_buffer(to_owners(summed_rows(expert_terms).astype(jnp.bfloat16)))
    result = hidden + gate[:, None] * expert_tok
    grad_result = cotangent.astype(jnp.float32).reshape(tok_rows, width)
    grad_expert_tok = (gate[:, None] * grad_result).astype(jnp.bfloat16)
    grad_gate = jnp.sum(grad_result * expert_tok, axis=-1)
    grad_logits = (
        router_probs * (jnp.where(chosen, grad_gate[:, None], 0.0) - (gate * grad_gate)[:, None])
    ).astype(jnp.bfloat16)
    grad_router = jnp.einsum("td,te->de", moe_in, grad_logits, preferred_element_type=jnp.float32)
    grad_rows = all_rows(to_experts(to_buffer(grad_expert_tok)))
    grad_act = jnp.einsum(
        "necd,efd->necf", grad_rows, expert_out, preferred_element_type=jnp.float32
    )
    grad_pre = gelu_pull(grad_act)[0].astype(jnp.bfloat16)
    grad_expert_out = jnp.einsum(
        "necf,necd->efd", expert_low, grad_rows, preferred_element_type=jnp.float32
    )
    grad_expert_in = jnp.einsum(
        "necd,necf->edf", expert_rows_in, grad_pre, preferred_element_type=jnp.float32
    )
    grad_back = jnp.einsum(
        "necf,edf->necd", grad_pre, expert_in, preferred_element_type=jnp.float32
    )
    grad_moe_in = from_buffer(to_owners(summed_rows(grad_back).astype(jnp.bfloat16)))
    grad_moe_in = grad_moe_in + jnp.einsum(
        "te,de->td", grad_logits, full_router, preferred_element_type=jnp.float32
    )
    grad_norm_moe, grad_gain_moe = norm_backward(grad_moe_in, hidden, inv_moe, gain_moe32)
    grad_hidden = grad_result + grad_norm_moe
    grad_branch = grad_hidden.astype(jnp.bfloat16)
    grad_out_w = jnp.einsum("te,td->ed", attn_tok, grad_branch, preferred_element_type=jnp.float32)
    grad_attn_tok = jnp.einsum(
        "td,ed->te", grad_branch, full_out, preferred_element_type=jnp.float32
    ).astype(jnp.bfloat16)
    grad_heads = to_heads(grad_attn_tok[:, None])[:, :, 0]
    delta = jnp.sum(grad_heads.astype(jnp.float32) * attn_heads.astype(jnp.float32), axis=-1)
    all_keys = lax.all_gather(keys, "blk", axis=0, tiled=True)
    all_values = lax.all_gather(values, "blk", axis=0, tiled=True)
    total_rows = all_keys.shape[0]
    step_rows = math.gcd(total_rows, group_rows)
    zero_heads = jnp.zeros((block_rows, seq_count, local_heads, HEAD_DIM), jnp.float32)
    zero_table = jnp.zeros(table32.shape, jnp.float32)

    def query_side(step_index, running):
        offset = step_index * step_rows
        key_block = lax.dynamic_slice_in_dim(all_keys, offset, step_rows, 0)
        value_block = lax.dynamic_slice_in_dim(all_values, offset, step_rows, 0)
        key_positions = offset + jnp.arange(step_rows, dtype=jnp.int32)

        def query_compute(current):
            grads = grad_step(
                queries,
                grad_heads,
                log_total,
                delta,
                query_positions,
                key_block,
                value_block,
                key_positions,
                seq_lengths,
                bounds,
                table32,
            )
            return (current[0] + grads[0], current[1] + grads[3])

        skipped = (offset > query_last) | (offset >= longest)
        return lax.cond(skipped, same_state, query_compute, running)

    grad_queries, grad_table = lax.fori_loop(
        0, total_rows // step_rows, query_side, (zero_heads, zero_table)
    )
    all_totals, all_deltas = (
        lax.all_gather(log_total, "blk", axis=0, tiled=True),
        lax.all_gather(delta, "blk", axis=0, tiled=True),
    )
    query_piece = lax.all_gather(queries, "blk", axis=0, tiled=True)
    grad_piece = lax.all_gather(grad_heads, "blk", axis=0, tiled=True)
    piece_rows = query_piece.shape[0]
    key_part_rows = math.gcd(piece_rows, group_rows)

    def key_one_part(step_index, inner_state):
        offset = step_index * key_part_rows
        query_part = lax.dynamic_slice_in_dim(query_piece, offset, key_part_rows, 0)
        grad_part = lax.dynamic_slice_in_dim(grad_piece, offset, key_part_rows, 0)
        total_part = lax.dynamic_slice_in_dim(all_totals, offset, key_part_rows, 0)
        delta_part = lax.dynamic_slice_in_dim(all_deltas, offset, key_part_rows, 0)
        part_positions = offset + jnp.arange(key_part_rows, dtype=jnp.int32)

        def key_compute(current):
            grads = grad_step(
                query_part,
                grad_part,
                total_part,
                delta_part,
                part_positions,
                keys,
                values,
                query_positions,
                seq_lengths,
                bounds,
                table32,
            )
            return (current[0] + grads[1], current[1] + grads[2])

        skipped = (offset + key_part_rows - 1 < query_first) | (query_first >= longest)
        return lax.cond(skipped, same_state, key_compute, inner_state)

    grad_keys, grad_values = lax.fori_loop(
        0, piece_rows // key_part_rows, key_one_part, (zero_heads, zero_heads)
    )
    grad_stack = jnp.stack((grad_queries, grad_keys, grad_values), axis=2).astype(jnp.bfloat16)
    grad_projected = to_tokens(grad_stack)
    grad_weights = jnp.einsum(
        "td,tce->cde", attn_in, grad_projected, preferred_element_type=jnp.float32
    )
    grad_attn_in = jnp.einsum(
        "tce,cde->td", grad_projected, stacked_weights, preferred_element_type=jnp.float32
    )
    grad_norm_attn, grad_gain_attn = norm_backward(grad_attn_in, source, inv_attn, gain_attn32)
    grad_tokens = grad_hidden + grad_norm_attn
    table_terms = lax.dynamic_update_slice_in_dim(
        jnp.zeros((NUM_BUCKETS, HEADS), jnp.float32), grad_table, head_index * local_heads, 1
    ).reshape(NUM_BUCKETS * HEADS)
    reduced = (
        lax.psum_scatter(grad_weights[0], ("head", "blk"), scatter_dimension=0, tiled=True),
        lax.psum_scatter(grad_weights[1], ("head", "blk"), scatter_dimension=0, tiled=True),
        lax.psum_scatter(grad_weights[2], ("head", "blk"), scatter_dimension=0, tiled=True),
        lax.psum_scatter(grad_out_w, ("head", "blk"), scatter_dimension=1, tiled=True),
        lax.psum_scatter(grad_gain_attn, ("head", "blk"), scatter_dimension=0, tiled=True),
        lax.psum_scatter(table_terms, ("head", "blk"), scatter_dimension=0, tiled=True),
        lax.psum_scatter(grad_gain_moe, ("head", "blk"), scatter_dimension=0, tiled=True),
        lax.psum_scatter(grad_router, ("head", "blk"), scatter_dimension=0, tiled=True),
    )
    return (
        result.astype(jnp.bfloat16).reshape(tokens.shape),
        grad_tokens.reshape(tokens.shape),
        reduced[4],
        reduced[0],
        reduced[1],
        reduced[2],
        reduced[3],
        reduced[5],
        reduced[6],
        reduced[7],
        grad_expert_in,
        grad_expert_out,
    )


def solution(mesh):
    in_specs = (
        P("blk", "head", None),
        P(("head", "blk")),
        P(("head", "blk"), None),
        P(("head", "blk"), None),
        P(("head", "blk"), None),
        P(None, ("head", "blk")),
        P(("head", "blk")),
        P(("head", "blk")),
        P(("head", "blk"), None),
        P("blk", None, "head"),
        P("blk", "head", None),
        P(),
        P(),
        P("head", "blk", None, None),
        P("blk", "head", None),
    )
    out_specs = (
        P("blk", "head", None),
        P("blk", "head", None),
        P(("head", "blk")),
        P(("head", "blk"), None),
        P(("head", "blk"), None),
        P(("head", "blk"), None),
        P(None, ("head", "blk")),
        P(("head", "blk")),
        P(("head", "blk")),
        P(("head", "blk"), None),
        P("blk", None, "head"),
        P("blk", "head", None),
    )
    return jax.shard_map(
        on_device, mesh=mesh, in_specs=in_specs, out_specs=out_specs, check_vma=False
    )
```

profile of v0, /device:TPU:8, one launch (start us, length us, event | category | flops | bytes accessed | tf_op | source)
XLA Modules:
  0.0 1444.4 jit_solution(8887634225672102340)
XLA Ops:
  12.0 40.8 %all-reduce.8 = (bf16[768]{0:T(1024)(128)(2,1)S(1)}, bf16[384]{0:T(512)(128)(2,1)S(1)}, bf16[768]{0:T(1024)(128)(2,1)S(1)}) all-reduce(bf16[768]{0:T(1024)(128)(2,1)S(1)} %dynamic-update-slice, bf16[384]{0:T(512)(128)(2,1)S(1)} %dynamic-update-slice.1, ...), channel_id=1, replica_groups=mesh['head'=4,'blk'=8] {'head','blk'}, use_global_device_ids=true, to_apply=%add | all-reduce | flops 1920 | bytes 7680
  65.4 56.0 %all-gather.17.cloned.1.call-done = bf16[768,768]{1,0:T(8,128)(2,1)} async-done(((bf16[24,768]{1,0:T(8,128)(2,1)}), bf16[768,768]{1,0:T(8,128)(2,1)}) %all-gather.17.cloned.1.call-update) | async-done | bytes 1179664 | tf_op jit(solution)/shard_map/all_gather | solution.py:157
  121.4 56.0 %all-gather.19.cloned.1.call-done = bf16[768,768]{1,0:T(8,128)(2,1)} async-done(((bf16[24,768]{1,0:T(8,128)(2,1)}), bf16[768,768]{1,0:T(8,128)(2,1)}) %all-gather.19.cloned.1.call-update) | async-done | bytes 1179664 | tf_op jit(solution)/shard_map/all_gather | solution.py:158
  181.4 18.3 %all_to_all.68 = bf16[256,1,3,4,192]{0,4,2,1,3:T(8,128)(2,1)S(1)} all-to-all(bf16[256,1,3,4,192]{0,4,2,1,3:T(8,128)(2,1)S(1)} %copy.152), channel_id=1, replica_groups=mesh['head'=4,'blk'=8] {'head'}, dimensions={3} | all-to-all | bytes 2359296 | tf_op jit(solution)/shard_map/all_to_all | solution.py:177
  208.5 53.7 %all-gather.29.cloned.1.call-done = bf16[2048,4,1,3,64]{0,4,3,2,1:T(8,128)(2,1)} async-done(((bf16[256,4,1,3,64]{0,4,3,2,1:T(8,128)(2,1)}), bf16[2048,4,1,3,64]{0,4,3,2,1:T(8,128)(2,1)}) %all-gather.29.cloned.1.call-update) | async-done | bytes 3145744 | tf_op jit(solution)/shard_map/all_gather | solution.py:202
  266.3 59.8 %all-gather.31.cloned.1.call-done = bf16[2048,4,1,3,64]{0,4,3,2,1:T(8,128)(2,1)} async-done(((bf16[256,4,1,3,64]{0,4,3,2,1:T(8,128)(2,1)}), bf16[2048,4,1,3,64]{0,4,3,2,1:T(8,128)(2,1)}) %all-gather.31.cloned.1.call-update) | async-done | bytes 3145744 | tf_op jit(solution)/shard_map/all_gather | solution.py:203
  326.7 39.7 %while.55 = (s32[]{:T(128)}, f32[3,4,256]{2,1,0:T(4,128)S(1)}, f32[3,4,256]{2,1,0:T(4,128)}, f32[256,4,3,64]{0,3,2,1:T(8,128)S(1)}, s32[]{:T(128)}, /*index=5*/s...) while((s32[]{:T(128)}, f32[3,4,256]{2,1,0:T(4,128)S(1)}, ...), condition=%wide.region_8.9_spmd.clone, body=%wide.region_3.8_spmd.clone.sunk | while | flops 228141568 | bytes 18015124 | solution.py:229
  327.4 11.3 conditional.10
  339.4 11.3 conditional.10
  386.3 72.8 %all_to_all.69 = bf16[8,1,48,768]{3,2,1,0:T(8,128)(2,1)} all-to-all(bf16[8,1,48,768]{3,2,1,0:T(8,128)(2,1)S(1)} %bitcast.328), channel_id=1, replica_groups=mesh['head'=4,'blk'=8] {'blk'}, dimensions={0} | all-to-all | bytes 1179648 | tf_op jit(solution)/shard_map/all_to_all | solution.py:268
  459.2 63.0 %all-gather.3 = bf16[32,24,8]{1,2,0:T(8,128)(2,1)S(1)} all-gather(bf16[1,24,8]{1,2,0:T(8,128)(2,1)S(1)} %bitcast.345), channel_id=1, replica_groups=mesh['head'=4,'blk'=8] {'head','blk'}, dimensions={0}, use_global_device_ids=true | all-gather | bytes 12672 | tf_op jit(solution)/shard_map/all_gather | solution.py:163
  525.2 19.5 %all_to_all.70 = bf16[8,1,48,768]{3,2,1,0:T(8,128)(2,1)} all-to-all(bf16[8,1,48,768]{3,2,1,0:T(8,128)(2,1)S(1)} %bitcast.329), channel_id=1, replica_groups=mesh['head'=4,'blk'=8] {'blk'}, dimensions={0} | all-to-all | bytes 1179648 | tf_op jit(solution)/shard_map/all_to_all | solution.py:268
  555.7 12.1 all-gather.25.cloned.1.call-done
  581.2 22.8 %reduce-scatter.14.cloned.1.call-done = bf16[8,1,48,768]{3,2,0,1:T(8,128)(2,1)} async-done(((bf16[32,1,48,768]{3,2,0,1:T(8,128)(2,1)}), bf16[8,1,48,768]{3,2,0,1:T(8,128)(2,1)}) %reduce-scatter.14.cloned.1.call-update) | async-done | bytes 589840 | tf_op jit(solution)/shard_map/reduce_scatter | solution.py:274
  610.0 30.1 %reduce-scatter.16.cloned.1.call-done = bf16[8,1,48,768]{3,2,0,1:T(8,128)(2,1)} async-done(((bf16[32,1,48,768]{3,2,0,1:T(8,128)(2,1)}), bf16[8,1,48,768]{3,2,0,1:T(8,128)(2,1)}) %reduce-scatter.16.cloned.1.call-update) | async-done | bytes 589840 | tf_op jit(solution)/shard_map/reduce_scatter | solution.py:274
  647.9 20.0 %all-to-all-done.5 = bf16[8,1,48,768]{3,2,1,0:T(8,128)(2,1)} async-done(((bf16[8,1,48,768]{3,2,1,0:T(8,128)(2,1)}), bf16[8,1,48,768]{3,2,1,0:T(8,128)(2,1)}, u32[]{:S(2)}, u32[]{:S(2)}) %all-to-all-start.5) | async-done | bytes 589856 | tf_op jit(solution)/shard_map/all_to_all | solution.py:279
  691.9 18.2 %all-gather.33.cloned.1.call-done = bf16[2048,4,1,3,64]{0,4,3,2,1:T(8,128)(2,1)} async-done(((bf16[256,4,1,3,64]{0,4,3,2,1:T(8,128)(2,1)}), bf16[2048,4,1,3,64]{0,4,3,2,1:T(8,128)(2,1)}) %all-gather.33.cloned.1.call-update) | async-done | bytes 3145744 | tf_op jit(solution)/shard_map/all_gather | solution.py:365
  714.8 32.3 %all_gather.63 = f32[2048,4,3]{0,1,2:T(4,128)} all-gather(f32[256,4,3]{0,1,2:T(4,128)} %bitcast.81), channel_id=1, replica_groups=mesh['head'=4,'blk'=8] {'blk'}, dimensions={0}, use_global_device_ids=true | all-gather | bytes 110592 | tf_op jit(solution)/shard_map/all_gather | solution.py:362
  749.4 104.0 %while.56 = (s32[]{:T(128)}, f32[256,4,3,64]{0,3,2,1:T(8,128)}, f32[32,3]{0,1:T(4,128)}, s32[]{:T(128)}, s32[]{:T(128)}, /*index=5*/s32[4]{0:T(128)}, bf16[2048,...) while((s32[]{:T(128)}, f32[256,4,3,64]{0,3,2,1:T(8,128)}, ...), condition=%wide.region_25.26_spmd.clone, body=%wide.region_21.25_spmd.clone.sunk | while | flops 402327136 | bytes 35218208 | solution.py:358
  759.4 29.5 %conditional.11 = ((f32[256,4,3,64]{0,3,2,1:T(8,128)}, f32[32,3]{0,1:T(4,128)})) conditional(s32[]{:T(128)} %convert_element_type.319, (s32[]{:T(128)}, s32[256]{0:T(256)S(1)}, s32[]{:T(128)}, s32[4]{0:T(128)}, bf16[2048,4,3,64]{0,3,1,2:T(8,128)(2,1)}, /*index=5*/bf16[256,4,3,64]{0,3,1,2:T(8,128)(2,1)S(1)}, s32[32]{0:T(128)}, s32[32]{0:T(128)}, ...), branch_computations={%region_22.23_spmd, %region_24.24_spmd} | conditional | flops 402327136 | bytes 35216836 | solution.py:356
  763.7 11.5 copy.141
  789.6 29.6 %conditional.11 = ((f32[256,4,3,64]{0,3,2,1:T(8,128)}, f32[32,3]{0,1:T(4,128)})) conditional(s32[]{:T(128)} %convert_element_type.319, (s32[]{:T(128)}, s32[256]{0:T(256)S(1)}, s32[]{:T(128)}, s32[4]{0:T(128)}, bf16[2048,4,3,64]{0,3,1,2:T(8,128)(2,1)}, /*index=5*/bf16[256,4,3,64]{0,3,1,2:T(8,128)(2,1)S(1)}, s32[32]{0:T(128)}, s32[32]{0:T(128)}, ...), branch_computations={%region_22.23_spmd, %region_24.24_spmd} | conditional | flops 402327136 | bytes 35216836 | solution.py:356
  794.0 11.5 copy.141
  819.9 29.5 %conditional.11 = ((f32[256,4,3,64]{0,3,2,1:T(8,128)}, f32[32,3]{0,1:T(4,128)})) conditional(s32[]{:T(128)} %convert_element_type.319, (s32[]{:T(128)}, s32[256]{0:T(256)S(1)}, s32[]{:T(128)}, s32[4]{0:T(128)}, bf16[2048,4,3,64]{0,3,1,2:T(8,128)(2,1)}, /*index=5*/bf16[256,4,3,64]{0,3,1,2:T(8,128)(2,1)S(1)}, s32[32]{0:T(128)}, s32[32]{0:T(128)}, ...), branch_computations={%region_22.23_spmd, %region_24.24_spmd} | conditional | flops 402327136 | bytes 35216836 | solution.py:356
  824.2 11.5 copy.141
  854.5 174.7 %all_gather.65 = f32[2048,4,3]{0,2,1:T(4,128)S(1)} all-gather(f32[256,4,3]{0,2,1:T(4,128)S(1)} %multiply_reduce_fusion.1), channel_id=1, replica_groups=mesh['head'=4,'blk'=8] {'blk'}, dimensions={0}, use_global_device_ids=true | all-gather | bytes 110592 | tf_op jit(solution)/shard_map/all_gather | solution.py:363
  1029.5 57.0 %while.57 = (s32[]{:T(128)}, f32[256,4,3,64]{0,3,2,1:T(8,128)S(1)}, f32[256,4,3,64]{0,3,2,1:T(8,128)S(1)}, s32[]{:T(128)}, pred[]{:T(512)}, /*index=5*/s32[4]{0:...) while((s32[]{:T(128)}, f32[256,4,3,64]{0,3,2,1:T(8,128)S(1)}, ...), condition=%wide.region_29.30_spmd.clone.clone, body=%wide.region_26.29_spmd.clone.clone.sunk | while | flops 430245376 | bytes 28279728 | solution.py:397
  1086.8 18.4 %all_to_all.72 = bf16[256,4,3,1,192]{0,4,2,3,1:T(8,128)(2,1)S(1)} all-to-all(bf16[256,4,3,1,192]{0,4,2,3,1:T(8,128)(2,1)S(1)} %pad_maximum_fusion.5), channel_id=1, replica_groups=mesh['head'=4,'blk'=8] {'head'}, dimensions={1} | all-to-all | bytes 2359296 | tf_op jit(solution)/shard_map/all_to_all | solution.py:183
  1136.2 57.9 %all-reduce.7 = (f32[768]{0:T(1024)S(1)}, f32[384]{0:T(512)S(1)}, f32[768]{0:T(1024)S(1)}, f32[768,8]{0,1:T(8,128)S(1)}) all-reduce(f32[768]{0:T(1024)} %get-tuple-element.1899, f32[384]{0:T(512)S(1)} %reshape.503, f32[768]{0:T(1024)S(1)} %copy-done.39, f32[768,8]{0,1:T(8,128)} %fusion.176), channel_id=7, replica_groups=mesh['head'=4,'blk'=8] {'head','blk'}, use_global_device_ids=true, to_apply=%region_32.33.clone | all-reduce | flops 8064 | bytes 64512
  1200.2 28.8 %reduce-scatter.20.cloned.1.call-done = f32[24,768]{1,0:T(8,128)} async-done(((f32[768,768]{1,0:T(8,128)}), f32[24,768]{1,0:T(8,128)}) %reduce-scatter.20.cloned.1.call-update) | async-done | bytes 73744
  1229.0 103.8 %reduce-scatter.22.cloned.1.call-done = f32[24,768]{1,0:T(8,128)} async-done(((f32[768,768]{1,0:T(8,128)}), f32[24,768]{1,0:T(8,128)}) %reduce-scatter.22.cloned.1.call-update) | async-done | bytes 73744
  1332.8 104.6 %reduce-scatter.24.cloned.1.call-done = f32[24,768]{1,0:T(8,128)} async-done(((f32[768,768]{1,0:T(8,128)}), f32[24,768]{1,0:T(8,128)}) %reduce-scatter.24.cloned.1.call-update) | async-done | bytes 73744
  (507 shorter events, 375.6 us)
Async XLA Ops:
  7.2 544.1 %copy-start = (bf16[1,768,768]{2,1,0:T(8,128)(2,1)S(1)}, bf16[1,768,768]{2,1,0:T(8,128)(2,1)}, u32[]{:S(2)}) copy-start(bf16[1,768,768]{2,1,0:T(8,128)(2,1)} %param.37) | copy-start | bytes 3538948
  7.2 58.2 %all-gather.15.cloned.1.call-start = ((), (), s32[]{:S(2)}) async-start(), calls=%async_computation.14 | async-start | bytes 1216512 | tf_op jit(solution)/shard_map/all_gather | solution.py:156
  7.9 113.5 %all-gather.17.cloned.1.call-start = ((), (), s32[]{:S(2)}) async-start(), calls=%async_computation.15 | async-start | bytes 1216512 | tf_op jit(solution)/shard_map/all_gather | solution.py:157
  8.7 168.7 %all-gather.19.cloned.1.call-start = ((), (), s32[]{:S(2)}) async-start(), calls=%async_computation.16 | async-start | bytes 1216512 | tf_op jit(solution)/shard_map/all_gather | solution.py:158
  9.4 252.9 %all-gather.29.cloned.1.call-start = ((), (), s32[]{:S(2)}) async-start(), calls=%async_computation.24 | async-start | bytes 3538944 | tf_op jit(solution)/shard_map/all_gather | solution.py:202
  52.8 124.6 %copy-start.30 = (f32[768]{0:T(1024)}, f32[768]{0:T(1024)S(1)}, u32[]{:S(2)}) copy-start(f32[768]{0:T(1024)S(1)} %convert_element_type.180) | copy-start | bytes 9220
  54.6 122.8 %copy-start.43 = (f32[256]{0:T(256)}, f32[256]{0:T(256)S(1)}, u32[]{:S(2)}) copy-start(f32[256]{0:T(256)S(1)} %get-tuple-element.2031) | copy-start | bytes 3076
  201.1 124.9 %all-gather.31.cloned.1.call-start = ((), (), s32[]{:S(2)}) async-start(), calls=%async_computation.25 | async-start | bytes 3538944 | tf_op jit(solution)/shard_map/all_gather | solution.py:203
  201.7 180.4 %all-gather.21.cloned.1.call-start = ((), (), s32[]{:S(2)}) async-start(), calls=%async_computation.17 | async-start | bytes 1216512 | tf_op jit(solution)/shard_map/all_gather | solution.py:159
  205.7 60.6 %copy-start.28 = (s32[8,2,128]{2,0,1:T(8,128)}, s32[8,2,128]{2,0,1:T(8,128)S(1)}, u32[]{:S(2)}) copy-start(s32[8,2,128]{2,0,1:T(8,128)S(1)} %reduce-window.6) | copy-start | bytes 24580
  368.0 14.1 all-to-all-start.1
  371.5 173.5 %all-gather.23.cloned.1.call-start = ((), (), s32[]{:S(2)}) async-start(), calls=%async_computation.18 | async-start | bytes 2949120 | tf_op jit(solution)/shard_map/all_gather | solution.py:271
  382.8 76.4 %copy-start.48 = (bf16[24,8]{0,1:T(8,128)(2,1)S(1)}, bf16[24,8]{0,1:T(8,128)(2,1)}, u32[]{:S(2)}) copy-start(bf16[24,8]{0,1:T(8,128)(2,1)} %param.35) | copy-start | bytes 1156
  382.8 140.8 %copy-start.33 = (s32[1,256,1,1]{1,3,2,0:T(1,128)S(1)}, s32[1,256,1,1]{1,3,2,0:T(1,128)}, u32[]{:S(2)}) copy-start(s32[1,256,1,1]{1,3,2,0:T(1,128)} %param.40) | copy-start | bytes 3076
  459.2 108.6 %all-gather.25.cloned.1.call-start = ((), (), s32[]{:S(2)}) async-start(), calls=%async_computation.20 | async-start | bytes 2949120 | tf_op jit(solution)/shard_map/all_gather | solution.py:271
  523.6 124.0 %copy-start.23 = (f32[256,8]{0,1:T(8,128)}, f32[256,8]{0,1:T(8,128)S(1)}, u32[]{:S(2)}) copy-start(f32[256,8]{0,1:T(8,128)S(1)} %get-tuple-element.2037) | copy-start | bytes 24580
  523.6 123.9 %copy-start.35 = (f32[256]{0:T(256)}, f32[256]{0:T(256)S(1)}, u32[]{:S(2)}) copy-start(f32[256]{0:T(256)S(1)} %get-tuple-element.2036) | copy-start | bytes 3076
  523.7 123.9 %copy-start.40 = (f32[256]{0:T(256)}, f32[256]{0:T(256)S(1)}, u32[]{:S(2)}) copy-start(f32[256]{0:T(256)S(1)} %fusion.163) | copy-start | bytes 3076
  544.7 59.3 %reduce-scatter.14.cloned.1.call-start = ((), (), s32[]{:S(2)}) async-start(), calls=%async_computation.19 | async-start | bytes 2949120 | tf_op jit(solution)/shard_map/reduce_scatter | solution.py:274
  555.6 84.6 %reduce-scatter.16.cloned.1.call-start = ((), (), s32[]{:S(2)}) async-start(), calls=%async_computation.21 | async-start | bytes 2949120 | tf_op jit(solution)/shard_map/reduce_scatter | solution.py:274
  580.4 65.8 %copy-start.14 = (bf16[256,1,768]{2,0,1:T(8,128)(2,1)S(1)}, bf16[256,1,768]{2,0,1:T(8,128)(2,1)}, u32[]{:S(2)}) copy-start(bf16[256,1,768]{2,0,1:T(8,128)(2,1)} %param.41) | copy-start | bytes 1179652
  580.5 129.7 %all-gather.33.cloned.1.call-start = ((), (), s32[]{:S(2)}) async-start(), calls=%async_computation.26 | async-start | bytes 3538944 | tf_op jit(solution)/shard_map/all_gather | solution.py:365
  604.0 36.2 %all-to-all-start.3 = ((bf16[8,1,48,768]{3,2,1,0:T(8,128)(2,1)}), bf16[8,1,48,768]{3,2,1,0:T(8,128)(2,1)S(1)}, u32[]{:S(2)}, u32[]{:S(2)}) async-start(bf16[8,1,48,768]{3,2,1,0:T(8,128)(2,1)} %bitcast.337), calls=%async_computation.4 | async-start | bytes 1179648 | tf_op jit(solution)/shard_map/all_to_all | solution.py:279
  640.2 27.7 %all-to-all-start.5 = ((bf16[8,1,48,768]{3,2,1,0:T(8,128)(2,1)}), bf16[8,1,48,768]{3,2,1,0:T(8,128)(2,1)}, u32[]{:S(2)}, u32[]{:S(2)}) async-start(bf16[8,1,48,768]{3,2,1,0:T(8,128)(2,1)} %bitcast.336), calls=%async_computation.7 | async-start | bytes 1179648 | tf_op jit(solution)/shard_map/all_to_all | solution.py:279
  646.2 383.1 %all-gather.27.cloned.1.call-start = ((), (), s32[]{:S(2)}) async-start(), calls=%async_computation.22 | async-start | bytes 3538944 | tf_op jit(solution)/shard_map/all_gather | solution.py:366
  647.6 23.8 %copy-start.37 = (f32[256]{0:T(256)}, f32[256]{0:T(256)S(1)}, u32[]{:S(2)}) copy-start(f32[256]{0:T(256)S(1)} %get-tuple-element.2038) | copy-start | bytes 3076
  682.7 517.6 %reduce-scatter.18.cloned.1.call-start = ((), (), s32[]{:S(2)}) async-start(), calls=%async_computation.23 | async-start | bytes 2433024 | tf_op jit(solution)/shard_map/reduce_scatter | solution.py:417
  684.7 544.3 %reduce-scatter.20.cloned.1.call-start = ((), (), s32[]{:S(2)}) async-start(), calls=%async_computation.27 | async-start | bytes 2433024
  1112.2 220.6 %reduce-scatter.22.cloned.1.call-start = ((), (), s32[]{:S(2)}) async-start(), calls=%async_computation.28 | async-start | bytes 2433024
  1115.4 322.0 %reduce-scatter.24.cloned.1.call-start = ((), (), s32[]{:S(2)}) async-start(), calls=%async_computation.29 | async-start | bytes 2433024
  1131.4 64.5 %copy-start.5 = (f32[256,768]{1,0:T(8,128)S(1)}, f32[256,768]{1,0:T(8,128)}, u32[]{:S(2)}) copy-start(f32[256,768]{1,0:T(8,128)} %copy-done.4) | copy-start | bytes 2359300
  1131.4 306.1 %copy-start.1 = (bf16[1,768,768]{2,1,0:T(8,128)(2,1)S(1)}, bf16[1,768,768]{2,1,0:T(8,128)(2,1)}, u32[]{:S(2)}) copy-start(bf16[1,768,768]{2,1,0:T(8,128)(2,1)} %param.37) | copy-start | bytes 3538948
  (65 other events, 330.3 us)
Sparse Core Ops, SparseCore 0:
  10.9 54.3 all-gather.14
  68.3 53.0 all-gather.16
  124.3 53.0 all-gather.18
  201.3 60.9 all-gather.28
  264.8 61.2 all-gather.30
  328.8 53.2 all-gather.20
  459.3 22.3 all-gather.22
  544.8 22.9 all-gather.24
  570.9 33.0 reduce-scatter.13
  607.1 33.0 reduce-scatter.15
  642.2 67.8 all-gather.32
  712.0 61.8 all-gather.26
  779.8 98.7 reduce-scatter.17
  1112.3 116.6 reduce-scatter.19
  1234.8 98.0 reduce-scatter.21
  1339.4 98.0 reduce-scatter.23
where the time goes:
time: 1460 us; the launch traced here: 1440 us
  waiting for transfers between devices  590 us (40%)
  blocking collectives  508 us (35%)
  matrix products  148 us (10%)
  local copies, waits for them, and re-layouts  105 us (7%)
  other arithmetic  38.9 us (3%)
  loops' own time  23 us (2%)
  starting transfers between devices  16.4 us (1%)
  between operations  15.8 us (1%)
    unnamed x19, waiting for transfers between devices  241 us
    all_gather x1, blocking collectives, on_device(): lax.all_gather(delta, 'blk', axis=0, tiled=True)  175 us
    unnamed x2, blocking collectives  98.7 us
    all_to_all x2, blocking collectives, to_experts(): lax.all_to_all(buffer, 'blk', split_axis=0, concat_axis=0, tiled=True)  92.3 us
    all_gather x1, blocking collectives, on_device(): lax.all_gather(w_router, ('head', 'blk'), axis=0, tiled=True)  63 us
    all_gather x1, waiting for transfers between devices, on_device(): value_piece = lax.all_gather(values, 'blk', axis=0, tiled=True)  59.8 us
    all_gather x1, waiting for transfers between devices, on_device(): lax.all_gather(w_value, ('head', 'blk'), axis=0, tiled=True)  56 us
    all_gather x1, waiting for transfers between devices, on_device(): lax.all_gather(w_key, ('head', 'blk'), axis=0, tiled=True)  56 us
  transfers between devices with their start and end apart: 19, of which 14 were waited for; matrix products, arithmetic and copies ran while one was open for 19% of the time, Pallas kernels for 0%

commit v1 on v0

--- a/solution.py
+++ b/solution.py
@@ -1,8 +1,11 @@
+import functools
 import math
 
 import jax
 import jax.numpy as jnp
 from jax import lax
+from jax.experimental import pallas as pl
+from jax.experimental.pallas import tpu as pltpu
 from jax.sharding import PartitionSpec as P
 
 HEADS = 12
@@ -436,6 +439,1010 @@
     )
 
 
+BF = jnp.bfloat16
+F4 = jnp.float32
+NEG = -1e30
+QB = 256
+TILE = 512
+LANES = 128
+
+
+def dot(left, right, left_dim=1, right_dim=0):
+    dims = (((left_dim,), (right_dim,)), ((), ()))
+    return lax.dot_general(left, right, dims, preferred_element_type=F4)
+
+
+def iota(shape, dim):
+    return lax.broadcasted_iota(jnp.int32, shape, dim)
+
+
+def vmem_call(body, scalars, args, outs, scratch=(), mem=40, flops=0):
+    nbytes = sum(math.prod(a.shape) * a.dtype.itemsize for a in tuple(args) + tuple(outs))
+    return pl.pallas_call(
+        body,
+        out_shape=tuple(outs),
+        in_specs=[pl.BlockSpec(memory_space=pltpu.SMEM)]
+        + [pl.BlockSpec(memory_space=pltpu.VMEM)] * len(args),
+        out_specs=tuple(pl.BlockSpec(memory_space=pltpu.VMEM) for _ in outs),
+        scratch_shapes=list(scratch),
+        compiler_params=pltpu.CompilerParams(vmem_limit_bytes=mem * 1024 * 1024),
+        cost_estimate=pl.CostEstimate(flops=flops, bytes_accessed=nbytes, transcendentals=0),
+    )(scalars, *args)
+
+
+def shaped(shape, dtype):
+    return jax.ShapeDtypeStruct(shape, dtype)
+
+
+def ring_block(step, own_blk, ring_len):
+    half = ring_len // 2
+    place = jnp.where((own_blk & 1) == 0, own_blk >> 1, ring_len - 1 - (own_blk >> 1))
+    place = (place + step) & (ring_len - 1)
+    return jnp.where(place < half, 2 * place, 2 * ring_len - 1 - 2 * place)
+
+
+def ring_steps(ring_len):
+    steps = [0]
+    for hop in range(1, ring_len // 2):
+        steps += [-hop, hop]
+    return steps + [ring_len // 2]
+
+
+def shared_turn(position_block):
+    return ((position_block & 1) + (position_block >> 1)) & 1
+
+
+def norm_scale(values):
+    return lax.rsqrt(jnp.mean(values * values, axis=-1, keepdims=True) + norm_eps)
+
+
+def head_tile(block, head, place):
+    tile = block[:, LANES * (head // 2) : LANES * (head // 2) + LANES].astype(F4)
+    return tile if head % 2 == place else pltpu.roll(tile, HEAD_DIM, 1)
+
+
+def pack_units(n, sc, wq, wk, wv, misc, *rest):
+    outs, buf = rest[:n], rest[n]
+    rows = wq.shape[0]
+    lane = iota((rows, LANES), 1)
+    buf[...] = jnp.zeros(buf.shape, F4)
+    for j in range(n):
+        pair, turn = j // 2, j % 2
+        for c, weight in enumerate((wq, wk, wv)):
+            own = head_tile(weight, 3 * pair + turn, 0)
+            both = head_tile(weight, 3 * pair + 2, 1)
+            buf[j, 0:rows, LANES * c : LANES * c + LANES] = jnp.where(lane < HEAD_DIM, own, both)
+        buf[j, 0:rows, 3 * LANES : 4 * LANES] = misc[...].astype(F4)
+    for k in range(n):
+        outs[k][...] = buf[sc[0] ^ k].astype(BF)
+
+
+def place_rows(sc, n, rows, parts, dest):
+    for kk, part in enumerate(parts):
+        for k in range(n):
+            first = pl.multiple_of(((sc[1] ^ kk) * n + (sc[0] ^ k)) * rows, 8)
+            dest[pl.ds(first, rows), :] = part[k].astype(F4)[0:rows]
+
+
+def unpack_units(n, rows, sc, p0, p1, p2, p3, unit_w, misc, misc_t, buf):
+    place_rows(sc, n, rows, (p0, p1, p2, p3), buf)
+    unit_w[...] = buf[:, 0 : 3 * LANES].astype(BF)
+    tail = buf[:, 3 * LANES : 4 * LANES]
+    misc[...] = tail.astype(BF)
+    misc_t[...] = jnp.transpose(tail)
+
+
+def unpack_rows(n, rows, sc, p0, p1, p2, p3, out, buf):
+    place_rows(sc, n, rows, (p0, p1, p2, p3), buf)
+    out[...] = buf[...].astype(BF)
+
+
+def unpack_stack(n, rows, sc, p0, p1, p2, p3, out, buf):
+    parts = (p0, p1, p2, p3)
+    width = p0.shape[-1]
+    for kk, part in enumerate(parts):
+        for k in range(n):
+            first = pl.multiple_of(((sc[1] ^ kk) * n + (sc[0] ^ k)) * rows, 8)
+            block = part[k].astype(F4)
+            for c in range(3):
+                buf[pl.ds(first, rows), c * width : (c + 1) * width] = block[c * rows : (c + 1) * rows]
+    out[...] = buf[...].astype(BF)
+
+
+def bias_strips(sc, windows, out):
+    row = iota((8, TILE), 0)
+    for unit in range(2):
+        out[unit, 0] = jnp.full((QB, QB), NEG, F4)
+        for far in range(windows.shape[1]):
+            flat = jnp.broadcast_to(windows[unit, far : far + 1, :], (8, TILE))
+            turned = flat
+            for c in range(1, 8):
+                turned = jnp.where(row == c, pltpu.roll(flat, c, 1), turned)
+            for group in range(QB // 8):
+                moved = turned if group == 0 else pltpu.roll(turned, 8 * group, 1)
+                strip = moved[:, QB:]
+                if far == 0:
+                    after = iota((8, QB), 1) >= iota((8, QB), 0) + 8 * group
+                    strip = jnp.where(after, strip, NEG)
+                out[unit, far + 1, 8 * group : 8 * group + 8, :] = strip
+
+
+def project_blocks(layout, sc, *refs):
+    count = sum(layout)
+    blocks, (misc_t, unit_w), outs = refs[:count], refs[count : count + 2], refs[count + 2 :]
+    gain = misc_t[0:1, :]
+    at = 0
+    for i, parts in enumerate(layout):
+        block = jnp.concatenate([blocks[at + q][...].astype(F4) for q in range(parts)], axis=0)
+        at += parts
+        normed = (block * norm_scale(block) * gain).astype(BF)
+        made = dot(normed, unit_w[...])
+        outs[3 * i][...] = normed
+        outs[3 * i + 1][...] = made.astype(BF)
+        outs[3 * i + 2][...] = jnp.transpose(made).astype(BF)
+
+
+def unit_operands(n, sc, rows_refs, cols_refs, key_own, key_both, query_t, key_t, value_t, value_r):
+    lane = iota((QB, LANES), 1)
+    row = iota((QB, LANES), 0)
+    for i, step in enumerate(ring_steps(n)):
+        first = pl.multiple_of(ring_block(step, sc[0], n) * QB, QB)
+        keys = rows_refs[i][:, LANES : 2 * LANES].astype(F4)
+        hidden_key = jnp.where(first + row < sc[2], 0.0, NEG)
+        own = jnp.where(lane < HEAD_DIM, keys, jnp.where(lane == HEAD_DIM, hidden_key, 0.0))
+        both = jnp.where(lane >= HEAD_DIM, keys, jnp.where(lane == 0, hidden_key, 0.0))
+        key_own[pl.ds(first, QB), :] = own.astype(BF)
+        key_both[pl.ds(first, QB), :] = both.astype(BF)
+        query_t[:, pl.ds(first, QB)] = cols_refs[i][0:LANES, :]
+        if key_t is not None:
+            key_t[:, pl.ds(first, QB)] = cols_refs[i][LANES : 2 * LANES, :]
+        if value_t is not None:
+            value_t[:, pl.ds(first, QB)] = cols_refs[i][2 * LANES : 3 * LANES, :]
+        if value_r is not None:
+            value_r[pl.ds(first, QB), :] = rows_refs[i][:, 2 * LANES : 3 * LANES]
+
+
+def unit_half(unit, half, other):
+    return jnp.concatenate([half, other] if unit == 0 else [other, half], axis=0)
+
+
+def ones_row(cols):
+    return jnp.where(iota((HEAD_DIM, cols), 0) == 0, 1.0, 0.0).astype(BF)
+
+
+def strip_tile(bias, unit, far, cols):
+    def piece(key_half, query_half):
+        return bias[unit, jnp.maximum(far + query_half - key_half, -1) + 1]
+
+    if cols == TILE:
+        return jnp.concatenate(
+            [
+                jnp.concatenate([piece(0, 0), piece(0, 1)], axis=1),
+                jnp.concatenate([piece(1, 0), piece(1, 1)], axis=1),
+            ],
+            axis=0,
+        )
+    return jnp.concatenate([piece(0, 0), piece(1, 0)], axis=0)
+
+
+def attend_units(n, sc, *refs):
+    rows_refs, cols_refs, bias = refs[0:n], refs[n : 2 * n], refs[2 * n]
+    outs = refs[2 * n + 1 : 3 * n + 1]
+    logs = refs[3 * n + 1]
+    key_own, key_both, query_t, value_t, heads = refs[3 * n + 2 :]
+    turn = sc[0] & 1
+    unit_operands(n, sc, rows_refs, cols_refs, key_own, key_both, query_t, None, value_t, None)
+    heads[...] = jnp.zeros(heads.shape, F4)
+    logs[...] = jnp.zeros(logs.shape, F4)
+
+    def one_tile(unit, first_block, cols, last):
+        key_ref = key_own if unit == 0 else key_both
+        lo = HEAD_DIM * unit
+        start = pl.multiple_of(first_block * QB, QB)
+        queries = unit_half(
+            unit, query_t[lo : lo + HEAD_DIM, pl.ds(start, cols)], ones_row(cols)
+        )
+
+        def step(part, state):
+            top, total, mixed = state
+            key_at = pl.multiple_of(part * TILE, TILE)
+            scores = dot(key_ref[pl.ds(key_at, TILE), :], queries)
+            scores = scores + strip_tile(bias, unit, first_block - 2 * part, cols)
+            new_top = jnp.maximum(top, jnp.max(scores, axis=0, keepdims=True))
+            weights = jnp.exp(scores - new_top)
+            decay = jnp.exp(top - new_top)
+            total = total * decay + jnp.sum(weights, axis=0, keepdims=True)
+            added = dot(value_t[lo : lo + HEAD_DIM, pl.ds(key_at, TILE)], weights.astype(BF))
+            return (new_top, total, mixed * decay + added)
+
+        zero = jnp.zeros((1, cols), F4)
+        top, total, mixed = lax.fori_loop(
+            0, last + 1, step, (zero + NEG, zero, jnp.zeros((HEAD_DIM, cols), F4))
+        )
+        made = mixed / total
+        log_total = top + jnp.log(total)
+        for q in range(cols // QB):
+            heads[first_block + q, lo : lo + HEAD_DIM, :] = made[:, q * QB : (q + 1) * QB]
+            logs[unit * n + first_block + q] = log_total[:, q * QB : (q + 1) * QB]
+
+    def own_tile(i, carry):
+        one_tile(0, 2 * i, TILE, i)
+        return carry
+
+    def both_tile(i, carry):
+        one_tile(1, 2 * i + ((i + turn) & 1), QB, i)
+        return carry
+
+    lax.fori_loop(0, n // 2, own_tile, 0)
+    lax.fori_loop(0, n // 2, both_tile, 0)
+    for k in range(n):
+        outs[k][...] = heads[sc[0] ^ k].astype(BF)
+
+
+def unit_grads(n, sc, *refs):
+    rows_refs, cols_refs, bias = refs[0:n], refs[n : 2 * n], refs[2 * n]
+    head_refs, grad_refs = refs[2 * n + 1 : 3 * n + 1], refs[3 * n + 1 : 4 * n + 1]
+    logs = refs[4 * n + 1]
+    outs = refs[4 * n + 2 : 5 * n + 2]
+    stacked, table = refs[5 * n + 2 : 5 * n + 4]
+    (key_own, key_both, query_t, key_t, value_r, grad_t, delta, grad_k, grad_v, strips) = refs[
+        5 * n + 4 :
+    ]
+    turn = sc[0] & 1
+    unit_operands(n, sc, rows_refs, cols_refs, key_own, key_both, query_t, key_t, None, value_r)
+    for k in range(n):
+        block = sc[0] ^ k
+        grads = grad_refs[k][...]
+        grad_t[:, pl.ds(pl.multiple_of(block * QB, QB), QB)] = grads
+        product = grads.astype(F4) * head_refs[k][...].astype(F4)
+        delta[block] = jnp.sum(product[0:HEAD_DIM], axis=0, keepdims=True)
+        delta[n + block] = jnp.sum(product[HEAD_DIM:], axis=0, keepdims=True)
+    grad_k[...] = jnp.zeros(grad_k.shape, F4)
+    grad_v[...] = jnp.zeros(grad_v.shape, F4)
+    strips[...] = jnp.zeros(strips.shape, F4)
+    stacked[...] = jnp.zeros(stacked.shape, BF)
+
+    def one_tile(unit, first_block, cols, last):
+        key_ref = key_own if unit == 0 else key_both
+        lo = HEAD_DIM * unit
+        start = pl.multiple_of(first_block * QB, QB)
+        nothing = jnp.zeros((HEAD_DIM, cols), BF)
+        raw_queries = query_t[lo : lo + HEAD_DIM, pl.ds(start, cols)]
+        queries = unit_half(unit, raw_queries, ones_row(cols))
+        plain = unit_half(unit, raw_queries, nothing)
+        grads = unit_half(unit, grad_t[lo : lo + HEAD_DIM, pl.ds(start, cols)], nothing)
+        parts = cols // QB
+        log_total = jnp.concatenate([logs[unit * n + first_block + q] for q in range(parts)], axis=1)
+        inner = jnp.concatenate([delta[unit * n + first_block + q] for q in range(parts)], axis=1)
+
+        def step(part, grad_q):
+            key_at = pl.multiple_of(part * TILE, TILE)
+            far = first_block - 2 * part
+            scores = dot(key_ref[pl.ds(key_at, TILE), :], queries)
+            scores = scores + strip_tile(bias, unit, far, cols)
+            probs = jnp.exp(scores - log_total)
+            grad_probs = dot(value_r[pl.ds(key_at, TILE), :], grads)
+            grad_scores = probs * (grad_probs - inner)
+            for key_half in range(2):
+                for q in range(parts):
+                    at = jnp.maximum(far + q - key_half, -1) + 1
+                    strips[unit, at] += grad_scores[
+                        key_half * QB : (key_half + 1) * QB, q * QB : (q + 1) * QB
+                    ]
+            low = grad_scores.astype(BF)
+            grad_v[pl.ds(key_at, TILE), :] += dot(probs.astype(BF), grads, 1, 1)
+            grad_k[pl.ds(key_at, TILE), :] += dot(low, plain, 1, 1)
+            return grad_q + dot(key_t[lo : lo + HEAD_DIM, pl.ds(key_at, TILE)], low)
+
+        grad_q = lax.fori_loop(0, last + 1, step, jnp.zeros((HEAD_DIM, cols), F4))
+        for q in range(parts):
+            stacked[first_block + q, lo : lo + HEAD_DIM, :] = grad_q[
+                :, q * QB : (q + 1) * QB
+            ].astype(BF)
+
+    def own_tile(i, carry):
+        one_tile(0, 2 * i, TILE, i)
+        return carry
+
+    def both_tile(i, carry):
+        one_tile(1, 2 * i + ((i + turn) & 1), QB, i)
+        return carry
+
+    lax.fori_loop(0, n // 2, both_tile, 0)
+    lax.fori_loop(0, n // 2, own_tile, 0)
+    for j in range(n):
+        stacked[j, LANES : 2 * LANES, :] = jnp.transpose(grad_k[QB * j : QB * j + QB, :]).astype(BF)
+        stacked[j, 2 * LANES :, :] = jnp.transpose(grad_v[QB * j : QB * j + QB, :]).astype(BF)
+    for k in range(n):
+        outs[k][...] = stacked[sc[0] ^ k]
+    row = iota((8, TILE), 0)
+    empty = jnp.zeros((8, QB), F4)
+    for unit in range(2):
+        for far in range(n):
+            total = jnp.zeros((8, TILE), F4)
+            for group in range(QB // 8):
+                rows8 = strips[unit, far + 1, 8 * group : 8 * group + 8, :]
+                wide = jnp.concatenate([empty, rows8], axis=1)
+                total = total + (wide if group == 0 else pltpu.roll(wide, TILE - 8 * group, 1))
+            lined = jnp.where(row == 0, total, 0.0)
+            for c in range(1, 8):
+                lined = lined + jnp.where(row == c, pltpu.roll(total, TILE - c, 1), 0.0)
+            table[unit * n + far] = jnp.sum(lined, axis=0, keepdims=True)
+
+
+def dispatch_rows(n, cap, sc, route_ref, cot, wo_t, *rest):
+    outs, target = rest[:n], rest[n]
+    tok = cot.shape[0]
+    rows = wo_t.shape[0]
+    route = route_ref[...]
+    chosen = iota((n, tok), 0) == route
+    upto = jnp.where(iota((tok, tok), 0) <= iota((tok, tok), 1), 1.0, 0.0).astype(BF)
+    filled = dot(jnp.where(chosen, 1.0, 0.0).astype(BF), upto)
+    slot = jnp.sum(jnp.where(chosen, filled - 1.0, 0.0), axis=0, keepdims=True)
+    place = (route ^ sc[0]) * cap + slot.astype(jnp.int32)
+    target[...] = jnp.broadcast_to(place, target.shape)
+    spread = jnp.where(iota((n * cap, tok), 0) == place, 1.0, 0.0).astype(BF)
+    packed = dot(spread, cot[...])
+    rest_rows = outs[0].shape[0] - cap - rows
+    tail = [wo_t[...].astype(F4), jnp.zeros((rest_rows, packed.shape[1]), F4)]
+    for k in range(n):
+        outs[k][...] = jnp.concatenate([packed[k * cap : (k + 1) * cap]] + tail, axis=0).astype(BF)
+
+
+def pair_rows(sc, n, refs, dest, place_own):
+    turn = sc[0] & 1
+    wanted = shared_turn(sc[0])
+    for m in range(n // 2):
+        pair = (sc[0] >> 1) ^ m
+        for k in (2 * m, 2 * m + 1):
+            head = 3 * pair + (turn ^ (k & 1))
+            place_own(pl.multiple_of(head * HEAD_DIM, HEAD_DIM), refs[k])
+        first = jnp.broadcast_to(turn == wanted, (HEAD_DIM, QB))
+        both = jnp.where(
+            first,
+            refs[2 * m][HEAD_DIM:LANES, :].astype(F4),
+            refs[2 * m + 1][HEAD_DIM:LANES, :].astype(F4),
+        )
+        dest[pl.ds(pl.multiple_of((3 * pair + 2) * HEAD_DIM, HEAD_DIM), HEAD_DIM), :] = both.astype(
+            dest.dtype
+        )
+
+
+def spread_matrix(target, rows):
+    place = target[0:1, :]
+    return jnp.where(iota((rows, place.shape[1]), 0) == place, 1.0, 0.0)
+
+
+def hidden_rows(n, cap, sc, *refs):
+    heads, (wo_t, tokens, misc_t, target) = refs[:n], refs[n : n + 4]
+    attn, hidden_out = refs[n + 4 : n + 6]
+    outs, buf = refs[n + 6 : 2 * n + 6], refs[2 * n + 6]
+
+    def place_own(at, ref):
+        buf[pl.ds(at, HEAD_DIM), :] = ref[0:HEAD_DIM, :].astype(F4)
+
+    pair_rows(sc, n, heads, buf, place_own)
+    rows = jnp.transpose(buf[...]).astype(BF)
+    attn[...] = rows
+    hidden = tokens[...].astype(F4) + dot(rows, wo_t[...], 1, 1)
+    hidden_out[...] = hidden
+    moe_in = (hidden * norm_scale(hidden) * misc_t[1:2, :]).astype(BF)
+    packed = dot(spread_matrix(target, n * cap).astype(BF), moe_in).astype(BF)
+    for k in range(n):
+        outs[k][...] = packed[k * cap : (k + 1) * cap]
+
+
+def gelu_pair(values):
+    scale = math.sqrt(2.0 / math.pi)
+    square = values * values
+    bend = jnp.tanh(scale * (values + 0.044715 * values * square))
+    act = 0.5 * values * (1.0 + bend)
+    slope = 0.5 * (1.0 + bend) + 0.5 * values * (1.0 - bend * bend) * scale * (
+        1.0 + 3.0 * 0.044715 * square
+    )
+    return (act, slope)
+
+
+def route_probs(experts, sc, rows, misc):
+    logits = dot(rows, misc[...])
+    lane = iota(logits.shape, 1)
+    real = (lane >= 2) & (lane < 2 + experts)
+    logits = jnp.where(real, logits, NEG)
+    powers = jnp.where(real, jnp.exp(logits - jnp.max(logits, axis=-1, keepdims=True)), 0.0)
+    probs = powers / jnp.sum(powers, axis=-1, keepdims=True)
+    chosen = lane == sc[0] + 2
+    gate = jnp.sum(jnp.where(chosen, probs, 0.0), axis=-1, keepdims=True)
+    return (probs, chosen, gate)
+
+
+def expert_back(experts, sc, rows_ref, cot_ref, in_a, in_b, out_a, out_b, misc, back, act_out, log_out, gate_out):
+    rows, cots = rows_ref[...], cot_ref[...]
+    probs, chosen, gate = route_probs(experts, sc, rows, misc)
+    gate_out[...] = jnp.broadcast_to(gate, gate_out.shape)
+    inner = jnp.zeros(gate.shape, F4)
+    width = in_a.shape[1]
+    total = jnp.zeros(rows.shape, F4)
+    for half, (w_in, w_out) in enumerate(((in_a, out_a), (in_b, out_b))):
+        act, slope = gelu_pair(dot(rows, w_in[...]))
+        low = act.astype(BF)
+        act_out[:, half * width : (half + 1) * width] = low
+        grad_act = dot(cots, w_out[...], 1, 1)
+        inner = inner + jnp.sum(low.astype(F4) * grad_act, axis=-1, keepdims=True)
+        total = total + dot((gate * grad_act * slope).astype(BF), w_in[...], 1, 1)
+    grad_logits = (inner * probs * (jnp.where(chosen, 1.0, 0.0) - gate)).astype(BF)
+    log_out[...] = grad_logits
+    back[...] = (total + dot(grad_logits, misc[...], 1, 1)).astype(back.dtype)
+
+
+def expert_forward(sc, act, gate, out_a, out_b, made):
+    width = out_a.shape[0]
+    total = dot(act[:, :width], out_a[...]) + dot(act[:, width:], out_b[...])
+    made[...] = (gate[:, 0:1] * total).astype(made.dtype)
+
+
+def expert_weights(experts, count, sc, *refs):
+    rows_refs, cot_refs = refs[:count], refs[count : 2 * count]
+    w_in, w_out, misc, grad_in, grad_out = refs[2 * count :]
+    for i in range(count):
+        rows, cots = rows_refs[i][...], cot_refs[i][...]
+        gate = route_probs(experts, sc, rows, misc)[2]
+        act, slope = gelu_pair(dot(rows, w_in[...]))
+        grads = (gate * cots.astype(F4)).astype(BF)
+        grad_pre = (dot(grads, w_out[...], 1, 1) * slope).astype(BF)
+        in_part = dot(rows, grad_pre, 0, 0)
+        out_part = dot(act.astype(BF), grads, 0, 0)
+        if i == 0:
+            grad_in[...] = in_part
+            grad_out[...] = out_part
+        else:
+            grad_in[...] += in_part
+            grad_out[...] += out_part
+
+
+def add_split(n, cap, extra, sc, own, other, *rest):
+    tails, outs = rest[:extra], rest[extra:]
+    total = own[...] + other[...].astype(F4)
+    tail = [t[...].astype(F4) for t in tails]
+    used = cap + sum(t.shape[0] for t in tail)
+    if outs[0].shape[0] > used:
+        tail.append(jnp.zeros((outs[0].shape[0] - used, total.shape[1]), F4))
+    for k in range(n):
+        outs[k][...] = jnp.concatenate([total[k * cap : (k + 1) * cap]] + tail, axis=0).astype(BF)
+
+
+def result_rows(n, cap, sc, *refs):
+    made, (target, hidden, out) = refs[:n], refs[n:]
+    rows = jnp.concatenate([made[k][0:cap, :] for k in range(n)], axis=0)
+    spread = jnp.transpose(spread_matrix(target, n * cap)).astype(BF)
+    out[...] = (hidden[...] + dot(spread, rows)).astype(BF)
+
+
+def norm_back(grads, source, gain):
+    scale = norm_scale(source)
+    weighted = grads * gain
+    inner = jnp.mean(weighted * source, axis=-1, keepdims=True)
+    return (scale * weighted - source * (scale * scale * scale) * inner, scale)
+
+
+def hidden_grads(n, cap, sc, *refs):
+    back, (target, hidden_ref, misc_t, cot, wo_t) = refs[:n], refs[n : n + 5]
+    grad_out, low_out, gain_out = refs[n + 5 : n + 8]
+    outs, buf = refs[n + 8 : 2 * n + 8], refs[2 * n + 8]
+    rows = jnp.concatenate([back[k][...] for k in range(n)], axis=0)
+    spread = jnp.transpose(spread_matrix(target, n * cap)).astype(BF)
+    grads = dot(spread, rows)
+    hidden = hidden_ref[...]
+    normed, scale = norm_back(grads, hidden, misc_t[1:2, :])
+    gain_out[...] = jnp.broadcast_to(
+        jnp.sum(grads * hidden * scale, axis=0, keepdims=True), gain_out.shape
+    )
+    total = cot[...].astype(F4) + normed
+    grad_out[...] = total
+    low = total.astype(BF)
+    low_out[...] = low
+    buf[...] = jnp.transpose(dot(low, wo_t[...])).astype(BF)
+    turn = sc[0] & 1
+    for k in range(n):
+        pair = (sc[0] >> 1) ^ (k >> 1)
+        own = pl.multiple_of((3 * pair + (turn ^ (k & 1))) * HEAD_DIM, HEAD_DIM)
+        both = pl.multiple_of((3 * pair + 2) * HEAD_DIM, HEAD_DIM)
+        outs[k][0:HEAD_DIM, :] = buf[pl.ds(own, HEAD_DIM), :]
+        outs[k][HEAD_DIM:, :] = buf[pl.ds(both, HEAD_DIM), :]
+
+
+def token_grads(n, sc, *refs):
+    grads, (weights, tokens, hidden_grad, misc_t, out, buf) = refs[:n], refs[n:]
+    inner = weights.shape[1] // 3
+
+    def place_own(at, ref):
+        buf[pl.ds(at, HEAD_DIM), :] = ref[0:HEAD_DIM, :].astype(F4)
+        for c in (1, 2):
+            buf[pl.ds(c * inner + at, HEAD_DIM), :] = ref[
+                c * LANES : c * LANES + HEAD_DIM, :
+            ].astype(F4)
+
+    pair_rows(sc, n, grads, buf, place_own)
+    for m in range(n // 2):
+        at = pl.multiple_of((3 * ((sc[0] >> 1) ^ m) + 2) * HEAD_DIM, HEAD_DIM)
+        for c in (1, 2):
+            lo = c * LANES + HEAD_DIM
+            buf[pl.ds(c * inner + at, HEAD_DIM), :] = grads[2 * m][lo : lo + HEAD_DIM, :].astype(
+                F4
+            ) + grads[2 * m + 1][lo : lo + HEAD_DIM, :].astype(F4)
+    made = jnp.transpose(dot(weights[...], buf[...].astype(BF)))
+    normed, unused = norm_back(made, tokens[...].astype(F4), misc_t[0:1, :])
+    out[...] = hidden_grad[...] + normed
+
+
+def unit_weight_grads(n, heads, sc, *refs):
+    normed, (stacked, table) = refs[:n], refs[n : n + 2]
+    outs, buf = refs[n + 2 : n + 2 + heads], refs[n + 2 + heads]
+    total = None
+    for i, step in enumerate(ring_steps(n)):
+        part = dot(stacked[ring_block(step, sc[0], n)], normed[i][...])
+        total = part if total is None else total + part
+    buf[...] = jnp.transpose(total)
+    rows = buf.shape[0] // heads
+    width = buf.shape[1]
+    for kk in range(heads):
+        to = sc[1] ^ kk
+        outs[kk][...] = jnp.concatenate(
+            [
+                buf[pl.ds(pl.multiple_of(to * rows, 8), rows), :],
+                table[pl.ds(pl.multiple_of(to * n, 8), n), :],
+                jnp.zeros((8, width), F4),
+            ],
+            axis=0,
+        ).astype(BF)
+
+
+def two_parts(values, gap):
+    high = values.astype(BF).astype(F4)
+    lane = iota(values.shape, 1)
+    low = pltpu.roll(jnp.where(lane < gap, values - high, 0.0), gap, 1)
+    return jnp.where(lane < gap, high, low)
+
+
+def one_part(values, gap):
+    return values + pltpu.roll(values, values.shape[1] - gap, 1)
+
+
+def unit_weight_sums(n, rows, sc, p0, p1, p2, p3, *rest):
+    outs, buf = rest[:n], rest[n]
+    buf[...] = (
+        (p0[...].astype(F4) + p1[...].astype(F4)) + (p2[...].astype(F4) + p3[...].astype(F4))
+    )
+    base = n * rows
+    for k in range(n):
+        to = sc[0] ^ k
+        entry = buf[pl.ds(base + to, 1), :]
+        entry = two_parts(jnp.broadcast_to(one_part(entry, 2), (8, entry.shape[1])), 2)
+        outs[k][...] = jnp.concatenate(
+            [buf[pl.ds(pl.multiple_of(to * rows, 8), rows), :], entry], axis=0
+        ).astype(BF)
+
+
+def unit_weight_final(n, sc, *refs):
+    parts, (wq, wk, wv, misc) = refs[:n], refs[n : n + 4]
+    grads, gain, table, buf = refs[n + 4 : n + 7], refs[n + 7], refs[n + 8], refs[n + 9]
+    rows = wq.shape[0]
+    for k in range(n):
+        buf[sc[0] ^ k] = parts[k][...].astype(F4)
+    lane = iota((rows, LANES), 1)
+    inner = jnp.zeros((rows, 1), F4)
+    for c, weight in enumerate((wq, wk, wv)):
+        lo = LANES * c
+
+        def piece(head, place):
+            pair, turn = head // 3, head % 3
+            if turn < 2:
+                tile, half = buf[2 * pair + turn, 0:rows, lo : lo + LANES], 0
+            else:
+                tile = (
+                    buf[2 * pair, 0:rows, lo : lo + LANES]
+                    + buf[2 * pair + 1, 0:rows, lo : lo + LANES]
+                )
+                half = 1
+            return tile if half == place else pltpu.roll(tile, HEAD_DIM, 1)
+
+        for m in range(weight.shape[1] // LANES):
+            tile = jnp.where(lane < HEAD_DIM, piece(2 * m, 0), piece(2 * m + 1, 1))
+            cols = slice(LANES * m, LANES * m + LANES)
+            grads[c][:, cols] = tile
+            inner = inner + jnp.sum(weight[:, cols].astype(F4) * tile, axis=-1, keepdims=True)
+    gain[...] = jnp.broadcast_to(inner / misc[:, 0:1].astype(F4), gain.shape)
+    for j in range(n):
+        table[j : j + 1, :] = one_part(buf[j, rows : rows + 1, 0:LANES], 2)
+
+
+def out_weight_grads(heads, sc, low, attn, rows_a, rows_b, logs_a, logs_b, gain, *rest):
+    outs, buf = rest[:heads], rest[heads]
+    width = attn.shape[1]
+    buf[:, 0:width] = dot(low[...], attn[...], 0, 0)
+    router = dot(rows_a[...], logs_a[...], 0, 0) + dot(rows_b[...], logs_b[...], 0, 0)
+    wide = jnp.where(iota((LANES, gain.shape[1]), 0) == 1, gain[0:1, :], 0.0)
+    buf[:, width : width + LANES] = two_parts(router + jnp.transpose(wide), 16)
+    rows = buf.shape[0] // heads
+    for kk in range(heads):
+        first = pl.multiple_of((sc[1] ^ kk) * rows, 8)
+        outs[kk][...] = buf[pl.ds(first, rows), :].astype(BF)
+
+
+def out_weight_sums(n, rows, sc, p0, p1, p2, p3, *rest):
+    outs, buf = rest[:n], rest[n]
+    width = buf.shape[1] - LANES
+    total = (p0[...].astype(F4) + p1[...].astype(F4)) + (p2[...].astype(F4) + p3[...].astype(F4))
+    buf[:, 0:width] = total[:, 0:width]
+    buf[:, width:] = two_parts(one_part(total[:, width:], 16), 16)
+    for k in range(n):
+        first = pl.multiple_of((sc[0] ^ k) * rows, 8)
+        outs[k][...] = jnp.concatenate(
+            [buf[pl.ds(first, rows), :], jnp.zeros((8, buf.shape[1]), F4)], axis=0
+        ).astype(BF)
+
+
+def out_weight_final(n, sc, *refs):
+    parts, (grad, extra) = refs[:n], refs[n:]
+    total = parts[0][...].astype(F4)
+    for k in range(1, n):
+        total = total + parts[k][...].astype(F4)
+    width = grad.shape[1]
+    grad[...] = total[0 : grad.shape[0], 0:width]
+    extra[...] = one_part(total[0 : grad.shape[0], width:], 16)
+
+
+def swap(values, axis, flip):
+    if flip == 0:
+        return values
+    size = lax.axis_size(axis)
+    return lax.ppermute(values, axis, [(i, i ^ flip) for i in range(size)])
+
+
+def exchange(messages, axis):
+    return [swap(message, axis, k) for k, message in enumerate(messages)]
+
+
+def after(values, earlier):
+    return lax.optimization_barrier((values, earlier))[0]
+
+
+def over_heads(stack):
+    across = swap(stack, "head", 2)
+    return (stack, swap(stack, "head", 1), across, swap(across, "head", 1))
+
+
+def on_plane(
+    tokens,
+    attn_gain,
+    w_query,
+    w_key,
+    w_value,
+    w_out,
+    bias_table,
+    moe_gain,
+    w_router,
+    expert_in,
+    expert_out,
+    seq_lengths,
+    rel_buckets,
+    routes,
+    cotangent,
+):
+    heads = lax.axis_size("head")
+    n = lax.axis_size("blk")
+    head_index = lax.axis_index("head")
+    blk = lax.axis_index("blk")
+    tok, width = tokens.shape[0], tokens.shape[2]
+    rows = w_query.shape[0]
+    total_rows = n * tok
+    experts = w_router.shape[1]
+    cap = 3 * tok // (2 * experts)
+    slots = n * cap
+    x = tokens.reshape(tok, width)
+    cot = cotangent.reshape(tok, width)
+    length = lax.dynamic_index_in_dim(seq_lengths, head_index, 0, False)
+    sc = jnp.stack([blk, head_index, length]).astype(jnp.int32)
+
+    def call(body, args, outs, scratch=(), mem=40, flops=0):
+        return vmem_call(body, sc, args, outs, scratch, mem, flops)
+
+    table_row = jnp.zeros((rows, HEADS), BF).at[0].set(bias_table)
+    misc_own = jnp.concatenate(
+        [
+            attn_gain[:, None],
+            moe_gain[:, None],
+            w_router,
+            jnp.zeros((rows, 16 - 2 - experts), BF),
+            table_row,
+            jnp.zeros((rows, LANES - 16 - HEADS), BF),
+        ],
+        axis=1,
+    )
+    unit_cols = 4 * LANES
+    packed = call(
+        functools.partial(pack_units, n),
+        (w_query, w_key, w_value, misc_own),
+        [shaped((rows + 8, unit_cols), BF)] * n,
+        [pltpu.VMEM((n, rows + 8, unit_cols), F4)],
+    )
+    unit_parts = over_heads(jnp.stack(exchange(packed, "blk")))
+    unit_w, misc, misc_t = call(
+        functools.partial(unpack_units, n, rows),
+        unit_parts,
+        [shaped((width, 3 * LANES), BF), shaped((width, LANES), BF), shaped((LANES, width), F4)],
+        [pltpu.VMEM((width, unit_cols), F4)],
+    )
+
+    order = [ring_of(i, n) for i in range(n)]
+    ahead = [(order[i], order[(i + 1) % n]) for i in range(n)]
+    astern = [(b, a) for a, b in ahead]
+    front = back = x
+    blocks = [(x,)]
+    for _ in range(n // 2 - 1):
+        front = lax.ppermute(front, "blk", ahead)
+        back = lax.ppermute(back, "blk", astern)
+        blocks += [(front,), (back,)]
+    half = tok // 2
+    blocks.append(
+        (
+            lax.ppermute(front[:half], "blk", ahead),
+            lax.ppermute(back[half:], "blk", astern),
+        )
+    )
+    normed, unit_rows, unit_cols_t = [], [], []
+    groups = [blocks[0:3], blocks[3:5], blocks[5:7], blocks[7:8]]
+    for group in groups:
+        made = call(
+            functools.partial(project_blocks, [len(g) for g in group]),
+            [part for g in group for part in g] + [misc_t, unit_w],
+            [
+                shaped((tok, width), BF),
+                shaped((tok, 3 * LANES), BF),
+                shaped((3 * LANES, tok), BF),
+            ]
+            * len(group),
+            flops=2 * len(group) * tok * width * 3 * LANES,
+        )
+        normed += made[0::3]
+        unit_rows += made[1::3]
+        unit_cols_t += made[2::3]
+
+    table_all = misc.reshape(heads * n, rows, LANES)[:, 0, 16 : 16 + HEADS].astype(F4)
+    pair, turn = blk // 2, blk % 2
+    own_col = lax.dynamic_index_in_dim(table_all, 3 * pair + turn, 1, False)
+    both_col = lax.dynamic_index_in_dim(table_all, 3 * pair + 2, 1, False)
+    labels = jnp.arange(NUM_BUCKETS, dtype=jnp.int32)
+    by_bucket = rel_buckets[None, :] == labels[:, None]
+    by_distance = jnp.stack(
+        [jnp.sum(jnp.where(by_bucket, col[:, None], 0.0), axis=0) for col in (own_col, both_col)]
+    )
+    shifted = jnp.pad(by_distance, ((0, 0), (QB, 0)))
+    windows = jnp.stack([shifted[:, QB * i : QB * i + TILE] for i in range(n)], axis=1)
+    (strips,) = call(bias_strips, (windows,), [shaped((2, n + 1, QB, QB), F4)])
+
+    wo_t = jnp.transpose(w_out)
+    extra = 80 if cap == 48 else -(-(cap + rows) // 16) * 16
+    cot_out = call(
+        functools.partial(dispatch_rows, n, cap),
+        (routes.reshape(1, tok), cot, wo_t),
+        [shaped((extra, width), BF)] * n + [shaped((8, tok), jnp.int32)],
+    )
+    target = cot_out[n]
+    cot_in = exchange([after(m, back) for m in cot_out[:n]], "blk")
+    cot_rows = jnp.concatenate([m[:cap] for m in cot_in])
+    (out_t,) = call(
+        functools.partial(unpack_rows, n, rows),
+        over_heads(jnp.stack([m[cap:] for m in cot_in])),
+        [shaped((width, width), BF)],
+        [pltpu.VMEM((width, width), F4)],
+    )
+    in_own, out_own = expert_in.reshape(expert_in.shape[1:]), expert_out.reshape(expert_out.shape[1:])
+    in_other = swap(after(in_own, unit_parts[2]), "head", 2)
+    out_other = swap(after(out_own, unit_parts[2]), "head", 2)
+
+    made = call(
+        functools.partial(attend_units, n),
+        list(unit_rows) + list(unit_cols_t) + [strips],
+        [shaped((LANES, tok), BF)] * n + [shaped((2 * n, 1, tok), F4)],
+        [
+            pltpu.VMEM((total_rows, LANES), BF),
+            pltpu.VMEM((total_rows, LANES), BF),
+            pltpu.VMEM((LANES, total_rows), BF),
+            pltpu.VMEM((LANES, total_rows), BF),
+            pltpu.VMEM((n, LANES, tok), F4),
+        ],
+        mem=48,
+        flops=10**9,
+    )
+    head_out, logs = made[:n], made[n]
+    head_in = exchange(head_out, "blk")
+    made = call(
+        functools.partial(hidden_rows, n, cap),
+        list(head_in) + [out_t, x, misc_t, target],
+        [shaped((tok, width), BF), shaped((tok, width), F4)] + [shaped((cap, width), BF)] * n,
+        [pltpu.VMEM((width, tok), F4)],
+        flops=4 * tok * width * width,
+    )
+    attn, hidden, moe_out = made[0], made[1], made[2:]
+
+    moe_rows = jnp.concatenate(exchange(moe_out, "blk"))
+    moe_pair = swap(moe_rows, "head", 1)
+    cot_pair = swap(cot_rows, "head", 1)
+
+    def backward_rows(rows_in, cots_in, kind):
+        return call(
+            functools.partial(expert_back, experts),
+            (rows_in, cots_in, in_own, in_other, out_own, out_other, misc),
+            [
+                shaped((slots, width), kind),
+                shaped((slots, 2 * width), BF),
+                shaped((slots, LANES), BF),
+                shaped((slots, LANES), F4),
+            ],
+            flops=12 * slots * width * width,
+        )
+
+    def forward_rows(act, gate, kind):
+        return call(
+            expert_forward,
+            (act, gate, out_own, out_other),
+            [shaped((slots, width), kind)],
+            flops=4 * slots * width * width,
+        )[0]
+
+    back_pair, act_pair, logs_pair, gate_pair = backward_rows(moe_pair, cot_pair, BF)
+    back_other = swap(back_pair, "head", 1)
+    back_own, act_own, logs_own, gate_own = backward_rows(moe_rows, cot_rows, F4)
+    back_out = call(
+        functools.partial(add_split, n, cap, 0),
+        (back_own, back_other),
+        [shaped((cap, width), BF)] * n,
+    )
+    back_in = exchange(back_out, "blk")
+    made = call(
+        functools.partial(hidden_grads, n, cap),
+        list(back_in) + [target, hidden, misc_t, cot, out_t],
+        [shaped((tok, width), F4), shaped((tok, width), BF), shaped((8, width), F4)]
+        + [shaped((LANES, tok), BF)] * n,
+        [pltpu.VMEM((width, tok), BF)],
+        flops=4 * tok * width * width,
+    )
+    grad_hidden, grad_low, gain_moe_part, grad_out_heads = made[0], made[1], made[2], made[3:]
+    grad_heads = exchange(grad_out_heads, "blk")
+
+    made = call(
+        functools.partial(unit_grads, n),
+        list(unit_rows) + list(unit_cols_t) + [strips] + list(head_out) + list(grad_heads) + [logs],
+        [shaped((3 * LANES, tok), BF)] * n
+        + [shaped((n, 3 * LANES, tok), BF), shaped((2 * n, 1, TILE), F4)],
+        [
+            pltpu.VMEM((total_rows, LANES), BF),
+            pltpu.VMEM((total_rows, LANES), BF),
+            pltpu.VMEM((LANES, total_rows), BF),
+            pltpu.VMEM((LANES, total_rows), BF),
+            pltpu.VMEM((total_rows, LANES), BF),
+            pltpu.VMEM((LANES, total_rows), BF),
+            pltpu.VMEM((2 * n, 1, tok), F4),
+            pltpu.VMEM((total_rows, LANES), F4),
+            pltpu.VMEM((total_rows, LANES), F4),
+            pltpu.VMEM((2, n + 1, QB, QB), F4),
+        ],
+        mem=56,
+        flops=3 * 10**9,
+    )
+    unit_out, stacked, lines = made[:n], made[n], made[n + 1]
+    unit_in = exchange(unit_out, "blk")
+
+    made_pair = forward_rows(act_pair, gate_pair, BF)
+    made_own = forward_rows(act_own, gate_own, F4)
+    tails = 3 * rows
+    res_out = call(
+        functools.partial(add_split, n, cap, 3),
+        (made_own, swap(made_pair, "head", 1), w_query, w_key, w_value),
+        [shaped((cap + tails + 8, width), BF)] * n,
+    )
+    res_out = [after(m, grad_heads[n - 1]) for m in res_out]
+    res_in = exchange(res_out, "blk")
+    (result,) = call(
+        functools.partial(result_rows, n, cap),
+        list(res_in) + [target, hidden],
+        [shaped((tok, width), BF)],
+    )
+    (full_w,) = call(
+        functools.partial(unpack_stack, n, rows),
+        over_heads(jnp.stack([m[cap:] for m in res_in])),
+        [shaped((width, 3 * width), BF)],
+        [pltpu.VMEM((width, 3 * width), F4)],
+    )
+    (grad_tokens,) = call(
+        functools.partial(token_grads, n),
+        list(unit_in) + [full_w, x, grad_hidden, misc_t],
+        [shaped((tok, width), F4)],
+        [pltpu.VMEM((3 * width, tok), F4)],
+    )
+
+    moe_far = swap(moe_rows, "head", 2)
+    cot_far = swap(after(cot_rows, out_other), "head", 2)
+    all_moe = (moe_rows, moe_pair, moe_far, swap(moe_far, "head", 1))
+    all_cot = (cot_rows, cot_pair, cot_far, swap(cot_far, "head", 1))
+    grad_in, grad_out = call(
+        functools.partial(expert_weights, experts, heads),
+        all_moe + all_cot + (in_own, out_own, misc),
+        [shaped(in_own.shape, F4), shaped(out_own.shape, F4)],
+        flops=8 * heads * slots * width * width,
+    )
+
+    wide = width + LANES
+    parts = call(
+        functools.partial(out_weight_grads, heads),
+        (grad_low, attn, moe_rows, moe_pair, logs_own, logs_pair, gain_moe_part),
+        [shaped((width // heads, wide), BF)] * heads,
+        [pltpu.VMEM((width, wide), F4)],
+        flops=2 * tok * width * width,
+    )
+    sums = call(
+        functools.partial(out_weight_sums, n, rows),
+        exchange(parts, "head"),
+        [shaped((rows + 8, wide), BF)] * n,
+        [pltpu.VMEM((width // heads, wide), F4)],
+    )
+    grad_out_t, small = call(
+        functools.partial(out_weight_final, n),
+        exchange(sums, "blk"),
+        [shaped((rows, width), F4), shaped((rows, LANES), F4)],
+    )
+
+    lines = lines.reshape(2, n, TILE)
+    near, far = lines[:, :, QB:], lines[:, :, :QB]
+    by_distance = near + jnp.pad(far[:, 1:], ((0, 0), (0, 1), (0, 0)))
+    by_distance = by_distance.reshape(2, total_rows)
+    table_part = jnp.sum(jnp.where(by_bucket[None], by_distance[:, None, :], 0.0), axis=2)
+    high = table_part.astype(BF).astype(F4)
+    table_part = jnp.concatenate([high, table_part - high]).T
+    table_part = jnp.pad(table_part, ((0, 0), (0, 3 * LANES - 4)))
+    parts = call(
+        functools.partial(unit_weight_grads, n, heads),
+        list(normed) + [stacked, table_part],
+        [shaped((width // heads + n + 8, 3 * LANES), BF)] * heads,
+        [pltpu.VMEM((width, 3 * LANES), F4)],
+        flops=2 * total_rows * width * 3 * LANES,
+    )
+    sums = call(
+        functools.partial(unit_weight_sums, n, rows),
+        exchange(parts, "head"),
+        [shaped((rows + 8, 3 * LANES), BF)] * n,
+        [pltpu.VMEM((width // heads + n + 8, 3 * LANES), F4)],
+    )
+    made = call(
+        functools.partial(unit_weight_final, n),
+        exchange(sums, "blk") + [w_query, w_key, w_value, misc_own],
+        [shaped((rows, width), F4)] * 3 + [shaped((rows, LANES), F4), shaped((n, LANES), F4)],
+        [pltpu.VMEM((n, rows + 8, 3 * LANES), F4)],
+    )
+    grad_q, grad_k, grad_v, gain_attn_grad, table_sum = made
+    own_sum, both_sum = table_sum[:, 0], table_sum[:, 1]
+    both_sum = both_sum.reshape(n // 2, 2).sum(axis=1, keepdims=True)
+    grad_table = jnp.concatenate([own_sum.reshape(n // 2, 2), both_sum], axis=1).reshape(HEADS)
+    return (
+        result.reshape(tokens.shape),
+        grad_tokens.reshape(tokens.shape),
+        gain_attn_grad[:, 0],
+        grad_q,
+        grad_k,
+        grad_v,
+        jnp.transpose(grad_out_t),
+        grad_table,
+        small[:, 1],
+        small[:, 2 : 2 + experts],
+        grad_in.reshape(expert_in.shape),
+        grad_out.reshape(expert_out.shape),
+    )
+
+
+def ring_of(place, ring_len):
+    return 2 * place if place < ring_len // 2 else 2 * ring_len - 1 - 2 * place
+
+
 def solution(mesh):
     in_specs = (
         P("blk", "head", None),
@@ -468,6 +1475,7 @@
         P("blk", None, "head"),
         P("blk", "head", None),
     )
+    one_each = mesh.shape["head"] == 4 and mesh.shape["blk"] == 8
     return jax.shard_map(
-        on_device, mesh=mesh, in_specs=in_specs, out_specs=out_specs, check_vma=False
-    )
+        on_plane if one_each else on_device, mesh=mesh, in_specs=in_specs, out_specs=out_specs, check_vma=False
+    )

time: 1460 us -> 459 us (0.31)
  blocking collectives: 508 us -> 0 us
  waiting for transfers between devices: 590 us -> 156 us
  matrix products: 148 us -> 0 us
  starting transfers between devices: 16.4 us -> 130 us
  Pallas kernels: 0 us -> 97.5 us
  local copies, waits for them, and re-layouts: 105 us -> 62.6 us
  other arithmetic: 38.9 us -> 2.01 us
  loops' own time: 23 us -> 0 us
    all_gather x10 -> x0, waiting for transfers between devices: 276 us -> none  [the longest x1 59.8 us: on_device(): value_piece = lax.all_gather(values, 'blk', axis=0, tiled=True)]
    all_gather x3 -> x0, blocking collectives: 270 us -> none  [the longest x1 175 us: on_device(): lax.all_gather(delta, 'blk', axis=0, tiled=True)]
    unnamed x19 -> x0, waiting for transfers between devices: 241 us -> none
    ppermute x0 -> x103, waiting for transfers between devices: none -> 156 us  [the longest x95 147 us: swap(): return lax.ppermute(values, axis, [(i, i ^ flip) for i in range(size)])]
    dot_general x73 -> x0, matrix products: 148 us -> none  [the longest x12 31.5 us: bias_terms(): jnp.einsum('qkb,bh->hqk', onehot, table32.astype(jnp.bfloat16), preferred...]
    all_to_all x5 -> x0, blocking collectives: 139 us -> none  [the longest x2 92.3 us: to_experts(): lax.all_to_all(buffer, 'blk', split_axis=0, concat_axis=0, tiled=True)]
    ppermute x0 -> x103, starting transfers between devices: none -> 130 us  [the longest x95 122 us: swap(): return lax.ppermute(values, axis, [(i, i ^ flip) for i in range(size)])]
    unnamed x2 -> x0, blocking collectives: 98.7 us -> none
  transfers between devices with their start and end apart: 19 -> 103, of which waited for: 14 -> 41; matrix products, arithmetic and copies ran while one was open for 19% -> 4% of each run, Pallas kernels for 0% -> 20%
where the time goes in v1:
time: 459 us; the launch traced here: 451 us
  waiting for transfers between devices  156 us (34%)
  starting transfers between devices  130 us (28%)
  Pallas kernels  97.5 us (21%)
  local copies, waits for them, and re-layouts  62.6 us (14%)
    ppermute x95, waiting for transfers between devices, swap(): return lax.ppermute(values, axis, [(i, i ^ flip) for i in range(size)])  147 us
    ppermute x95, starting transfers between devices, swap(): return lax.ppermute(values, axis, [(i, i ^ flip) for i in range(size)])  122 us
    pallas_call x29, Pallas kernels, vmem_call(): pl.pallas_call(body, out_shape=tuple(outs), in_specs=[pl.BlockSpec(memory...  97.5 us
    unnamed x349, local copies, waits for them, and re-layouts  54.4 us
  transfers between devices with their start and end apart: 103, of which 41 were waited for; matrix products, arithmetic and copies ran while one was open for 4% of the time, Pallas kernels for 20%

profile of v1, /device:TPU:8, one launch (start us, length us, event | category | flops | bytes accessed | tf_op | source)
XLA Modules:
  0.0 450.5 jit_solution(6517667560805851003)
XLA Ops:
  8.7 3.1 collective-permute-start.2
  26.1 4.4 collective-permute-done.10.p2
  30.5 3.3 collective-permute-start.13
  58.7 8.8 %collective-permute-done.14.refs_0_ = bf16[256,768]{1,0:T(8,128)(2,1)S(1)} collective-permute-done((bf16[256,768]{1,0:T(8,128)(2,1)S(1)}, bf16[256,768]{1,0:T(8,128)(2,1)S(1)}, u32[]{:S(2)}, u32[]{:S(2)}) %collective-permute-start.14) | collective-permute-done | bytes 393248 | tf_op jit(solution)/shard_map/ppermute | solution.py:1182
  72.8 3.4 collective-permute-start.28
  76.2 4.6 %collective-permute-done.26 = bf16[80,768]{1,0:T(8,128)(2,1)S(1)} collective-permute-done((bf16[80,768]{1,0:T(8,128)(2,1)S(1)}, bf16[80,768]{1,0:T(8,128)(2,1)S(1)}, u32[]{:S(2)}, u32[]{:S(2)}) %collective-permute-start.26) | collective-permute-done | bytes 122912 | tf_op jit(solution)/shard_map/ppermute | solution.py:1098
  86.1 4.0 collective-permute-done.29
  90.1 4.1 collective-permute-done.30
  98.6 9.9 %collective-permute-done.33.p2 = bf16[8,32,768]{2,1,0:T(8,128)(2,1)S(1)} collective-permute-done((bf16[8,32,768]{2,1,0:T(8,128)(2,1)S(1)}, bf16[8,32,768]{2,1,0:T(8,128)(2,1)S(1)}, u32[]{:S(2)}, u32[]{:S(2)}) %collective-permute-start.33) | collective-permute-done | bytes 393248 | tf_op jit(solution)/shard_map/ppermute | solution.py:1098
  110.5 14.6 %shard_map.245 = (bf16[128,256]{1,0:T(8,128)(2,1)S(1)}, bf16[128,256]{1,0:T(8,128)(2,1)S(1)}, bf16[128,256]{1,0:T(8,128)(2,1)S(1)}, bf16[128,256]{1,0:T(8,128)(2...) custom-call(s32[3]{0:T(128)S(1)} %pad_add_fusion.sc, ...), custom_call_target="tpu_custom_call" | custom-call | flops 1000000000 | bytes 8404992 | tf_op jit(solution)/shard_map/pallas_call | solution.py:461
  125.6 3.2 collective-permute-start.20
  146.1 3.1 collective-permute-done.35
  162.7 3.2 collective-permute-done.41
  166.0 22.8 %collective-permute-done.43.out_b = bf16[768,768]{1,0:T(8,128)(2,1)S(1)} collective-permute-done((bf16[768,768]{1,0:T(8,128)(2,1)S(1)}, bf16[768,768]{1,0:T(8,128)(2,1)S(1)}, u32[]{:S(2)}, u32[]{:S(2)}) %collective-permute-start.43) | collective-permute-done | bytes 1179680 | tf_op jit(solution)/shard_map/ppermute | solution.py:1098
  188.9 5.0 %shard_map.251 = (bf16[384,768]{1,0:T(8,128)(2,1)S(1)}, bf16[384,1536]{1,0:T(8,128)(2,1)S(1)}, bf16[384,128]{1,0:T(8,128)(2,1)S(1)}, f32[384,128]{1,0:T(8,128)S(1)}) custom-call(s32[3]{0:T(128)S(1)} %pad_add_fusion.sc, bf16[384,768]{1,0:T(8,128)(2,1)S(1)} %collective-permute-done.44.rows_ref.rows_b.refs_1_, ...), custom_call_target="tpu_custom_call" | custom-call | flops 2717908992 | bytes 8159232 | tf_op jit(solution)/shard_map/pallas_call | solution.py:461
  194.0 5.0 %shard_map.249 = (f32[384,768]{1,0:T(8,128)S(1)}, bf16[384,1536]{1,0:T(8,128)(2,1)S(1)}, bf16[384,128]{1,0:T(8,128)(2,1)S(1)}, f32[384,128]{1,0:T(8,128)S(1)}) custom-call(s32[3]{0:T(128)S(1)} %pad_add_fusion.sc, bf16[384,768]{1,0:T(8,128)(2,1)S(1)} %constant_dynamic-update-slice_fusion.16.rows_ref.rows_a.refs_0_, ...), custom_call_target="tpu_custom_call" | custom-call | flops 2717908992 | bytes 8749056 | tf_op jit(solution)/shard_map/pallas_call | solution.py:461
  212.1 12.3 %collective-permute-start.53 = (bf16[48,768]{1,0:T(8,128)(2,1)S(1)}, bf16[48,768]{1,0:T(8,128)(2,1)S(1)}, u32[]{:S(2)}, u32[]{:S(2)}) collective-permute-start(bf16[48,768]{1,0:T(8,128)(2,1)S(1)} %get-tuple-element.259), channel_id=1, source_target_pairs={{0,6},{1,7},{2,4},{3,5},{4,2},{5,3},{6,0},{7,1},{8,14},{9,15},{10,... | collective-permute-start | bytes 221192 | tf_op jit(solution)/shard_map/ppermute | solution.py:1098
  224.9 3.3 collective-permute-done.53.refs_6_
  236.4 4.2 collective-permute-start.64
  252.9 22.5 %shard_map.257 = (bf16[384,256]{1,0:T(8,128)(2,1)}, bf16[384,256]{1,0:T(8,128)(2,1)}, bf16[384,256]{1,0:T(8,128)(2,1)}, bf16[384,256]{1,0:T(8,128)(2,1)}, bf16[3...) custom-call(s32[3]{0:T(128)} %copy-done.46, ...), custom_call_target="tpu_custom_call" | custom-call | flops 3000000000 | bytes 12107776 | tf_op jit(solution)/shard_map/pallas_call | solution.py:461
  285.4 10.1 %collective-permute-done.59.refs_4_ = bf16[128,768]{1,0:T(8,128)(2,1)S(1)} collective-permute-done((bf16[128,768]{1,0:T(8,128)(2,1)S(1)}, bf16[128,768]{1,0:T(8,128)(2,1)S(1)}, u32[]{:S(2)}, u32[]{:S(2)}) %collective-permute-start.59) | collective-permute-done | bytes 196640 | tf_op jit(solution)/shard_map/ppermute | solution.py:1098
  301.1 8.5 %collective-permute-done.61.refs_6_ = bf16[128,768]{1,0:T(8,128)(2,1)S(1)} collective-permute-done((bf16[128,768]{1,0:T(8,128)(2,1)S(1)}, bf16[128,768]{1,0:T(8,128)(2,1)S(1)}, u32[]{:S(2)}, u32[]{:S(2)}) %collective-permute-start.61) | collective-permute-done | bytes 196640 | tf_op jit(solution)/shard_map/ppermute | solution.py:1098
  310.9 3.2 collective-permute-done.62.refs_7_
  334.3 9.4 %collective-permute-done.80.p2 = bf16[208,384]{1,0:T(8,128)(2,1)S(1)} collective-permute-done((bf16[208,384]{1,0:T(8,128)(2,1)S(1)}, bf16[208,384]{1,0:T(8,128)(2,1)S(1)}, u32[]{:S(2)}, u32[]{:S(2)}) %collective-permute-start.80) | collective-permute-done | bytes 159776 | tf_op jit(solution)/shard_map/ppermute | solution.py:1098
  352.9 3.8 collective-permute-done.83.refs_2_
  357.2 4.3 collective-permute-done.84.refs_3_
  362.2 4.0 collective-permute-done.85.refs_4_
  373.7 3.6 collective-permute-start.70
  378.4 14.7 %shard_map.266 = (f32[768,768]{1,0:T(8,128)}, f32[768,768]{1,0:T(8,128)}) custom-call(s32[3]{0:T(128)S(1)} %copy-done.47, bf16[384,768]{1,0:T(8,128)(2,1)S(1)} %copy-done.7, bf16[384,768]{1,0:T(8,128)(2,1)S(1)} %copy-done.9, bf16[384,768]{1,0:T(8,128)(2,1)} %collective-permute-done.99.refs_2_, bf16[384,768]{1,0:T(8,128)(2,1)} %collective-permute-done.100.refs_3_, ...), custom_call_target="tpu_custom_call" | custom-call | flops 7247757312 | bytes 11993088 | tf_op jit(solution)/shard_map/pallas_call | solution.py:461
  409.1 3.5 collective-permute-start.71
  413.9 3.7 collective-permute-start.73
  438.5 5.4 %collective-permute-done.74.refs_6_ = bf16[384,256]{1,0:T(8,128)(2,1)S(1)} collective-permute-done((bf16[384,256]{1,0:T(8,128)(2,1)}, bf16[384,256]{1,0:T(8,128)(2,1)S(1)}, u32[]{:S(2)}, u32[]{:S(2)}) %collective-permute-start.74) | collective-permute-done | bytes 196640 | tf_op jit(solution)/shard_map/ppermute | solution.py:1098
  (601 shorter events, 228.7 us)
Async XLA Ops:
  0.6 29.8 %collective-permute-start.1 = (bf16[256,768]{1,0:T(8,128)(2,1)}, bf16[256,768]{1,0:T(8,128)(2,1)S(1)}, u32[]{:S(2)}, u32[]{:S(2)}) collective-permute-start(bf16[256,768]{1,0:T(8,128)(2,1)} %bitcast.127), channel_id=1, source_target_pairs={{2,0},{4,2},{6,4},{7,6},{5,7},{3,5},{1,3},{0,1},{10,8},{12,10},{14... | collective-permute-start | bytes 1179656 | tf_op jit(solution)/shard_map/ppermute | solution.py:1183
  67.6 40.8 %collective-permute-start.16 = (bf16[128,768]{1,0:T(8,128)(2,1)S(1)}, bf16[128,768]{1,0:T(8,128)(2,1)S(1)}, u32[]{:S(2)}, u32[]{:S(2)}) collective-permute-start(bf16[128,768]{1,0:T(8,128)(2,1)S(1)} %slice.191), channel_id=1, source_target_pairs={{0,2},{2,4},{4,6},{6,7},{7,5},{5,3},{3,1},{1,0},{8,10},{10,12},{12... | collective-permute-start | bytes 589832 | tf_op jit(solution)/shard_map/ppermute | solution.py:1188
  68.0 40.5 %collective-permute-start.17 = (bf16[128,768]{1,0:T(8,128)(2,1)S(1)}, bf16[128,768]{1,0:T(8,128)(2,1)S(1)}, u32[]{:S(2)}, u32[]{:S(2)}) collective-permute-start(bf16[128,768]{1,0:T(8,128)(2,1)S(1)} %slice.192), channel_id=1, source_target_pairs={{2,0},{4,2},{6,4},{7,6},{5,7},{3,5},{1,3},{0,1},{10,8},{12,10},{14... | collective-permute-start | bytes 589832 | tf_op jit(solution)/shard_map/ppermute | solution.py:1189
  96.9 35.5 %collective-permute-start.32 = (bf16[8,32,768]{2,1,0:T(8,128)(2,1)S(1)}, bf16[8,32,768]{2,1,0:T(8,128)(2,1)S(1)}, u32[]{:S(2)}, u32[]{:S(2)}) collective-permute-start(bf16[8,32,768]{2,1,0:T(8,128)(2,1)S(1)} %constant_dynamic-update-slice_fusion.8.p0), channel_id=1, source_target_pairs={{0,8},{8,0},{16,24},{24,16},{1,9},{9,1},{17,25},{25,17},{2,10},{10... | collective-permute-start | bytes 1179656 | tf_op jit(solution)/shard_map/ppermute | solution.py:1098
  108.4 25.4 %collective-permute-start.34 = (bf16[8,32,768]{2,1,0:T(8,128)(2,1)S(1)}, bf16[8,32,768]{2,1,0:T(8,128)(2,1)S(1)}, u32[]{:S(2)}, u32[]{:S(2)}) collective-permute-start(bf16[8,32,768]{2,1,0:T(8,128)(2,1)S(1)} %collective-permute-done.33.p2), channel_id=1, source_target_pairs={{0,8},{8,0},{16,24},{24,16},{1,9},{9,1},{17,25},{25,17},{2,10},{10... | collective-permute-start | bytes 1179656 | tf_op jit(solution)/shard_map/ppermute | solution.py:1098
  137.1 28.9 %collective-permute-start.42 = (bf16[768,768]{1,0:T(8,128)(2,1)S(1)}, bf16[768,768]{1,0:T(8,128)(2,1)S(1)}, u32[]{:S(2)}, u32[]{:S(2)}) collective-permute-start(bf16[768,768]{1,0:T(8,128)(2,1)S(1)} %bitcast.138), channel_id=1, source_target_pairs={{0,16},{8,24},{16,0},{24,8},{1,17},{9,25},{17,1},{25,9},{2,18},{10... | collective-permute-start | bytes 3538952 | tf_op jit(solution)/shard_map/ppermute | solution.py:1098
  138.7 50.2 %collective-permute-start.43 = (bf16[768,768]{1,0:T(8,128)(2,1)S(1)}, bf16[768,768]{1,0:T(8,128)(2,1)S(1)}, u32[]{:S(2)}, u32[]{:S(2)}) collective-permute-start(bf16[768,768]{1,0:T(8,128)(2,1)S(1)} %bitcast.121), channel_id=1, source_target_pairs={{0,16},{8,24},{16,0},{24,8},{1,17},{9,25},{17,1},{25,9},{2,18},{10... | collective-permute-start | bytes 3538952 | tf_op jit(solution)/shard_map/ppermute | solution.py:1098
  139.2 49.7 %collective-permute-start.45 = (bf16[384,768]{1,0:T(8,128)(2,1)S(1)}, bf16[384,768]{1,0:T(8,128)(2,1)S(1)}, u32[]{:S(2)}, u32[]{:S(2)}) collective-permute-start(bf16[384,768]{1,0:T(8,128)(2,1)S(1)} %constant_dynamic-update-slice_fusion.24.cot_ref.refs_4_), channel_id=1, source_target_pairs={{0,8},{8,0},{16,24},{24,16},{1,9},{9,1},{17,25},{25,17},{2,10},{10... | collective-permute-start | bytes 1769480 | tf_op jit(solution)/shard_map/ppermute | solution.py:1098
  165.9 23.0 %collective-permute-start.44 = (bf16[384,768]{1,0:T(8,128)(2,1)S(1)}, bf16[384,768]{1,0:T(8,128)(2,1)S(1)}, u32[]{:S(2)}, u32[]{:S(2)}) collective-permute-start(bf16[384,768]{1,0:T(8,128)(2,1)S(1)} %constant_dynamic-update-slice_fusion.16.rows_ref.rows_a.refs_0_), channel_id=1, source_target_pairs={{0,8},{8,0},{16,24},{24,16},{1,9},{9,1},{17,25},{25,17},{2,10},{10... | collective-permute-start | bytes 1769480 | tf_op jit(solution)/shard_map/ppermute | solution.py:1098
  202.2 34.2 %collective-permute-start.101 = (bf16[384,768]{1,0:T(8,128)(2,1)S(1)}, bf16[384,768]{1,0:T(8,128)(2,1)}, u32[]{:S(2)}, u32[]{:S(2)}) collective-permute-start(bf16[384,768]{1,0:T(8,128)(2,1)S(1)} %constant_dynamic-update-slice_fusion.24.cot_ref.refs_4_), channel_id=1, source_target_pairs={{0,16},{8,24},{16,0},{24,8},{1,17},{9,25},{17,1},{25,9},{2,18},{10... | collective-permute-start | bytes 1769480 | tf_op jit(solution)/shard_map/ppermute | solution.py:1098
  203.8 36.8 %collective-permute-start.99 = (bf16[384,768]{1,0:T(8,128)(2,1)S(1)}, bf16[384,768]{1,0:T(8,128)(2,1)}, u32[]{:S(2)}, u32[]{:S(2)}) collective-permute-start(bf16[384,768]{1,0:T(8,128)(2,1)S(1)} %constant_dynamic-update-slice_fusion.16.rows_ref.rows_a.refs_0_), channel_id=1, source_target_pairs={{0,16},{8,24},{16,0},{24,8},{1,17},{9,25},{17,1},{25,9},{2,18},{10... | collective-permute-start | bytes 1769480 | tf_op jit(solution)/shard_map/ppermute | solution.py:1098
  209.7 31.4 %collective-permute-start.46 = (bf16[384,768]{1,0:T(8,128)(2,1)S(1)}, bf16[384,768]{1,0:T(8,128)(2,1)S(1)}, u32[]{:S(2)}, u32[]{:S(2)}) collective-permute-start(bf16[384,768]{1,0:T(8,128)(2,1)S(1)} %shard_map.252), channel_id=1, source_target_pairs={{0,8},{8,0},{16,24},{24,16},{1,9},{9,1},{17,25},{25,17},{2,10},{10... | collective-permute-start | bytes 1769480 | tf_op jit(solution)/shard_map/ppermute | solution.py:1098
  248.4 82.4 %collective-permute-start.102 = (bf16[384,768]{1,0:T(8,128)(2,1)}, bf16[384,768]{1,0:T(8,128)(2,1)}, u32[]{:S(2)}, u32[]{:S(2)}) collective-permute-start(bf16[384,768]{1,0:T(8,128)(2,1)} %collective-permute-done.101.refs_6_), channel_id=1, source_target_pairs={{0,8},{8,0},{16,24},{24,16},{1,9},{9,1},{17,25},{25,17},{2,10},{10... | collective-permute-start | bytes 1769480 | tf_op jit(solution)/shard_map/ppermute | solution.py:1098
  248.5 100.5 %collective-permute-start.100 = (bf16[384,768]{1,0:T(8,128)(2,1)}, bf16[384,768]{1,0:T(8,128)(2,1)}, u32[]{:S(2)}, u32[]{:S(2)}) collective-permute-start(bf16[384,768]{1,0:T(8,128)(2,1)} %collective-permute-done.99.refs_2_), channel_id=1, source_target_pairs={{0,8},{8,0},{16,24},{24,16},{1,9},{9,1},{17,25},{25,17},{2,10},{10... | collective-permute-start | bytes 1769480 | tf_op jit(solution)/shard_map/ppermute | solution.py:1098
  249.0 28.0 %collective-permute-start.56 = (bf16[128,768]{1,0:T(8,128)(2,1)S(1)}, bf16[128,768]{1,0:T(8,128)(2,1)S(1)}, u32[]{:S(2)}, u32[]{:S(2)}) collective-permute-start(bf16[128,768]{1,0:T(8,128)(2,1)S(1)} %get-tuple-element.265), channel_id=1, source_target_pairs={{0,1},{1,0},{2,3},{3,2},{4,5},{5,4},{6,7},{7,6},{8,9},{9,8},{10,11... | collective-permute-start | bytes 589832 | tf_op jit(solution)/shard_map/ppermute | solution.py:1098
  250.1 30.6 %collective-permute-start.57 = (bf16[128,768]{1,0:T(8,128)(2,1)S(1)}, bf16[128,768]{1,0:T(8,128)(2,1)S(1)}, u32[]{:S(2)}, u32[]{:S(2)}) collective-permute-start(bf16[128,768]{1,0:T(8,128)(2,1)S(1)} %get-tuple-element.267), channel_id=1, source_target_pairs={{0,2},{1,3},{2,0},{3,1},{4,6},{5,7},{6,4},{7,5},{8,10},{9,11},{10,... | collective-permute-start | bytes 589832 | tf_op jit(solution)/shard_map/ppermute | solution.py:1098
  252.3 30.8 %collective-permute-start.58 = (bf16[128,768]{1,0:T(8,128)(2,1)S(1)}, bf16[128,768]{1,0:T(8,128)(2,1)S(1)}, u32[]{:S(2)}, u32[]{:S(2)}) collective-permute-start(bf16[128,768]{1,0:T(8,128)(2,1)S(1)} %get-tuple-element.269), channel_id=1, source_target_pairs={{0,3},{1,2},{2,1},{3,0},{4,7},{5,6},{6,5},{7,4},{8,11},{9,10},{10,... | collective-permute-start | bytes 589832 | tf_op jit(solution)/shard_map/ppermute | solution.py:1098
  283.1 26.5 %collective-permute-start.61 = (bf16[128,768]{1,0:T(8,128)(2,1)S(1)}, bf16[128,768]{1,0:T(8,128)(2,1)S(1)}, u32[]{:S(2)}, u32[]{:S(2)}) collective-permute-start(bf16[128,768]{1,0:T(8,128)(2,1)S(1)} %get-tuple-element.275), channel_id=1, source_target_pairs={{0,6},{1,7},{2,4},{3,5},{4,2},{5,3},{6,0},{7,1},{8,14},{9,15},{10,... | collective-permute-start | bytes 589832 | tf_op jit(solution)/shard_map/ppermute | solution.py:1098
  315.5 50.8 %collective-permute-start.77 = (bf16[8,80,768]{2,1,0:T(8,128)(2,1)}, bf16[8,80,768]{2,1,0:T(8,128)(2,1)}, u32[]{:S(2)}, u32[]{:S(2)}) collective-permute-start(bf16[8,80,768]{2,1,0:T(8,128)(2,1)} %fusion.p0), channel_id=1, source_target_pairs={{0,16},{8,24},{16,0},{24,8},{1,17},{9,25},{17,1},{25,9},{2,18},{10... | collective-permute-start | bytes 2949128 | tf_op jit(solution)/shard_map/ppermute | solution.py:1098
  333.9 32.9 %collective-permute-start.89 = (bf16[192,896]{1,0:T(8,128)(2,1)S(1)}, bf16[192,896]{1,0:T(8,128)(2,1)S(1)}, u32[]{:S(2)}, u32[]{:S(2)}) collective-permute-start(bf16[192,896]{1,0:T(8,128)(2,1)S(1)} %get-tuple-element.327), channel_id=1, source_target_pairs={{0,8},{8,0},{16,24},{24,16},{1,9},{9,1},{17,25},{25,17},{2,10},{10... | collective-permute-start | bytes 1032200 | tf_op jit(solution)/shard_map/ppermute | solution.py:1098
  343.7 24.2 %collective-permute-start.90 = (bf16[192,896]{1,0:T(8,128)(2,1)S(1)}, bf16[192,896]{1,0:T(8,128)(2,1)S(1)}, u32[]{:S(2)}, u32[]{:S(2)}) collective-permute-start(bf16[192,896]{1,0:T(8,128)(2,1)S(1)} %get-tuple-element.328), channel_id=1, source_target_pairs={{0,16},{8,24},{16,0},{24,8},{1,17},{9,25},{17,1},{25,9},{2,18},{10... | collective-permute-start | bytes 1032200 | tf_op jit(solution)/shard_map/ppermute | solution.py:1098
  346.2 22.6 %collective-permute-start.91 = (bf16[192,896]{1,0:T(8,128)(2,1)S(1)}, bf16[192,896]{1,0:T(8,128)(2,1)S(1)}, u32[]{:S(2)}, u32[]{:S(2)}) collective-permute-start(bf16[192,896]{1,0:T(8,128)(2,1)S(1)} %get-tuple-element.329), channel_id=1, source_target_pairs={{0,24},{8,16},{16,8},{24,0},{1,25},{9,17},{17,9},{25,1},{2,26},{10... | collective-permute-start | bytes 1032200 | tf_op jit(solution)/shard_map/ppermute | solution.py:1098
  366.2 51.4 %collective-permute-start.76 = (bf16[8,80,768]{2,1,0:T(8,128)(2,1)}, bf16[8,80,768]{2,1,0:T(8,128)(2,1)}, u32[]{:S(2)}, u32[]{:S(2)}) collective-permute-start(bf16[8,80,768]{2,1,0:T(8,128)(2,1)} %fusion.p0), channel_id=1, source_target_pairs={{0,8},{8,0},{16,24},{24,16},{1,9},{9,1},{17,25},{25,17},{2,10},{10... | collective-permute-start | bytes 2949128 | tf_op jit(solution)/shard_map/ppermute | solution.py:1098
  366.2 52.5 %collective-permute-start.78 = (bf16[8,80,768]{2,1,0:T(8,128)(2,1)}, bf16[8,80,768]{2,1,0:T(8,128)(2,1)}, u32[]{:S(2)}, u32[]{:S(2)}) collective-permute-start(bf16[8,80,768]{2,1,0:T(8,128)(2,1)} %collective-permute-done.77.p2), channel_id=1, source_target_pairs={{0,8},{8,0},{16,24},{24,16},{1,9},{9,1},{17,25},{25,17},{2,10},{10... | collective-permute-start | bytes 2949128 | tf_op jit(solution)/shard_map/ppermute | solution.py:1098
  372.6 22.3 %collective-permute-start.69 = (bf16[384,256]{1,0:T(8,128)(2,1)S(1)}, bf16[384,256]{1,0:T(8,128)(2,1)S(1)}, u32[]{:S(2)}, u32[]{:S(2)}) collective-permute-start(bf16[384,256]{1,0:T(8,128)(2,1)S(1)} %copy-done.146), channel_id=1, source_target_pairs={{0,1},{1,0},{2,3},{3,2},{4,5},{5,4},{6,7},{7,6},{8,9},{9,8},{10,11... | collective-permute-start | bytes 589832 | tf_op jit(solution)/shard_map/ppermute | solution.py:1098
  373.7 22.8 %collective-permute-start.70 = (bf16[384,256]{1,0:T(8,128)(2,1)S(1)}, bf16[384,256]{1,0:T(8,128)(2,1)S(1)}, u32[]{:S(2)}, u32[]{:S(2)}) collective-permute-start(bf16[384,256]{1,0:T(8,128)(2,1)S(1)} %copy-done.145), channel_id=1, source_target_pairs={{0,2},{1,3},{2,0},{3,1},{4,6},{5,7},{6,4},{7,5},{8,10},{9,11},{10,... | collective-permute-start | bytes 589832 | tf_op jit(solution)/shard_map/ppermute | solution.py:1098
  377.3 21.5 %collective-permute-start.92 = (bf16[32,896]{1,0:T(8,128)(2,1)S(1)}, bf16[32,896]{1,0:T(8,128)(2,1)S(1)}, u32[]{:S(2)}, u32[]{:S(2)}) collective-permute-start(bf16[32,896]{1,0:T(8,128)(2,1)S(1)} %get-tuple-element.331), channel_id=1, source_target_pairs={{0,1},{1,0},{2,3},{3,2},{4,5},{5,4},{6,7},{7,6},{8,9},{9,8},{10,11... | collective-permute-start | bytes 172040 | tf_op jit(solution)/shard_map/ppermute | solution.py:1098
  409.1 26.5 %collective-permute-start.71 = (bf16[384,256]{1,0:T(8,128)(2,1)}, bf16[384,256]{1,0:T(8,128)(2,1)S(1)}, u32[]{:S(2)}, u32[]{:S(2)}) collective-permute-start(bf16[384,256]{1,0:T(8,128)(2,1)} %get-tuple-element.289), channel_id=1, source_target_pairs={{0,3},{1,2},{2,1},{3,0},{4,7},{5,6},{6,5},{7,4},{8,11},{9,10},{10,... | collective-permute-start | bytes 589832 | tf_op jit(solution)/shard_map/ppermute | solution.py:1098
  413.2 22.4 %collective-permute-start.72 = (bf16[384,256]{1,0:T(8,128)(2,1)}, bf16[384,256]{1,0:T(8,128)(2,1)S(1)}, u32[]{:S(2)}, u32[]{:S(2)}) collective-permute-start(bf16[384,256]{1,0:T(8,128)(2,1)} %get-tuple-element.290), channel_id=1, source_target_pairs={{0,4},{1,5},{2,6},{3,7},{4,0},{5,1},{6,2},{7,3},{8,12},{9,13},{10,... | collective-permute-start | bytes 589832 | tf_op jit(solution)/shard_map/ppermute | solution.py:1098
  413.9 24.6 %collective-permute-start.73 = (bf16[384,256]{1,0:T(8,128)(2,1)}, bf16[384,256]{1,0:T(8,128)(2,1)S(1)}, u32[]{:S(2)}, u32[]{:S(2)}) collective-permute-start(bf16[384,256]{1,0:T(8,128)(2,1)} %get-tuple-element.291), channel_id=1, source_target_pairs={{0,5},{1,4},{2,7},{3,6},{4,1},{5,0},{6,3},{7,2},{8,13},{9,12},{10,... | collective-permute-start | bytes 589832 | tf_op jit(solution)/shard_map/ppermute | solution.py:1098
  417.6 26.3 %collective-permute-start.74 = (bf16[384,256]{1,0:T(8,128)(2,1)}, bf16[384,256]{1,0:T(8,128)(2,1)S(1)}, u32[]{:S(2)}, u32[]{:S(2)}) collective-permute-start(bf16[384,256]{1,0:T(8,128)(2,1)} %get-tuple-element.292), channel_id=1, source_target_pairs={{0,6},{1,7},{2,4},{3,5},{4,2},{5,3},{6,0},{7,1},{8,14},{9,15},{10,... | collective-permute-start | bytes 589832 | tf_op jit(solution)/shard_map/ppermute | solution.py:1098
  418.7 27.7 %collective-permute-start.75 = (bf16[384,256]{1,0:T(8,128)(2,1)}, bf16[384,256]{1,0:T(8,128)(2,1)S(1)}, u32[]{:S(2)}, u32[]{:S(2)}) collective-permute-start(bf16[384,256]{1,0:T(8,128)(2,1)} %get-tuple-element.293), channel_id=1, source_target_pairs={{0,7},{1,6},{2,5},{3,4},{4,3},{5,2},{6,1},{7,0},{8,15},{9,14},{10,... | collective-permute-start | bytes 589832 | tf_op jit(solution)/shard_map/ppermute | solution.py:1098
  (225 other events, 2795.8 us)
